TPU v7x, 256 devices: a whole 4x4x8 slice. The times are simulated.
256 devices in a mesh: ep: 64 (over x_lo, y, z), dp: 4 (over x_hi, core).
Axes of the slice: x: 4 (x_hi: 2, x_lo: 2; x = x_hi * 2 + x_lo), y: 4, z: 8, core: 2. Of those that a mesh axis runs over, the one named last changes fastest.
Arguments:
- tokens: bfloat16 [32768, 3584], P(('ep', 'dp')), may hold values from -6 to 6
- cotangent: bfloat16 [32768, 3584], P(('ep', 'dp')), may hold values from -6 to 6
- routes: int32 [32768, 1], P(('ep', 'dp')), may hold values from 0 to 63; in each aligned block of 128 rows (0 to 127, 128 to 255, ...) at most 3 rows name the same one
- router_probs: float32 [32768, 1], P(('ep', 'dp')), may hold values from 0.1 to 1
- up_weight: bfloat16 [64, 3584, 1024], P('ep', None, 'dp'), may hold values from -0.09375 to 0.09375
- down_weight: bfloat16 [64, 1024, 3584], P('ep', 'dp'), may hold values from -0.1875 to 0.1875
- moving: int32 [32], replicated, may hold values 0 or 1
Outputs:
- outputs: bfloat16 [32768, 3584], P(('ep', 'dp'))
- input_grad: bfloat16 [32768, 3584], P(('ep', 'dp'))
- up_grad: bfloat16 [64, 3584, 1024], P('ep', None, 'dp')
- down_grad: bfloat16 [64, 1024, 3584], P('ep', 'dp')
Inputs may be any that keep to these rules, and one draw needn't show every extreme that they name: `routes`: within each device's aligned block of 128 rows, no expert is named by more than 3 rows, a bound that some block reaches.
All inputs are finite; a program needn't handle non-finite values.
Results may differ from a plain program's by a relative error of at most 0.0095.
Values may be sent and summed in bfloat16 or wider, within the bound.
A program may use at most 128 MiB of HBM per device.

v0:
```python
import jax
import jax.numpy as jnp
from jax import lax
from jax.sharding import PartitionSpec as P


def swapped_2(value, axis, bit):
    return lax.ppermute(value, axis, [(i, i ^ 1 << bit) for i in range(lax.axis_size(axis))])


def silu_grad(preact):
    sigmoid = jax.nn.sigmoid(preact)
    return sigmoid * (1.0 + preact * (1.0 - sigmoid))


def contract_rows(left, right):
    return lax.dot_general(
        left, right, (((0,), (0,)), ((), ())), preferred_element_type=jnp.float32
    )


def contract_cols(left, right):
    return lax.dot_general(
        left, right, (((1,), (1,)), ((), ())), preferred_element_type=jnp.float32
    )


def shards(tokens, cotangent, routes, router_probs, up_weight, down_weight, moving):
    ep_count = lax.axis_size("ep")
    dp_count = lax.axis_size("dp")
    half_count = ep_count // 2
    high_bit = ep_count.bit_length() - 2
    token_count = tokens.shape[0]
    feature_count = tokens.shape[1]
    capacity = 3 * token_count * routes.shape[1] // (2 * ep_count)
    slot_count = ep_count * capacity
    ep_index = lax.axis_index("ep")
    pair_ids = jnp.arange(half_count, dtype=jnp.int32)
    swapped = jnp.sum(jnp.where(pair_ids == ep_index % half_count, moving, 0)) == 1
    expert_of = routes[:, 0]
    router_weight = router_probs[:, 0]
    expert_flip = (
        jnp.sum(
            jnp.where((expert_of % half_count)[:, None] == pair_ids[None, :], moving[None, :], 0),
            axis=1,
        )
        == 1
    )
    partner = jnp.where(expert_of < half_count, expert_of + half_count, expert_of - half_count)
    target = jnp.where(expert_flip, partner, expert_of)
    other_up, other_down = swapped_2((up_weight, down_weight), "ep", high_bit)
    up_matrix = jnp.where(swapped, other_up, up_weight)[0]
    down_matrix = jnp.where(swapped, other_down, down_weight)[0]
    order = jnp.arange(token_count, dtype=jnp.int32)
    slot_rank = jnp.sum(
        ((target[:, None] == target[None, :]) & (order[None, :] < order[:, None])).astype(jnp.int32),
        axis=1,
    )
    slot_of = target * capacity + slot_rank
    select = (jnp.arange(slot_count, dtype=jnp.int32)[:, None] == slot_of[None, :]).astype(
        jnp.bfloat16
    )
    scaled_grad = (router_weight[:, None] * cotangent.astype(jnp.float32)).astype(jnp.bfloat16)
    token_buffer = jnp.dot(select, tokens, preferred_element_type=jnp.float32).astype(jnp.bfloat16)
    grad_buffer = jnp.dot(select, scaled_grad, preferred_element_type=jnp.float32).astype(
        jnp.bfloat16
    )
    token_buffer = token_buffer.reshape(ep_count, capacity, feature_count)
    grad_buffer = grad_buffer.reshape(ep_count, capacity, feature_count)
    arrived, arrived_grad = (
        lax.all_to_all(token_buffer, "ep", split_axis=0, concat_axis=0, tiled=True),
        lax.all_to_all(grad_buffer, "ep", split_axis=0, concat_axis=0, tiled=True),
    )
    routed, routed_grad = (
        lax.all_gather(arrived, "dp", axis=0, tiled=True),
        lax.all_gather(arrived_grad, "dp", axis=0, tiled=True),
    )
    row_count = dp_count * slot_count
    routed = routed.reshape(row_count, feature_count)
    routed_grad = routed_grad.reshape(row_count, feature_count)
    preact = jnp.dot(routed, up_matrix, preferred_element_type=jnp.float32)
    hidden = jax.nn.silu(preact).astype(jnp.bfloat16)
    out_part = jnp.dot(hidden, down_matrix, preferred_element_type=jnp.float32)
    out_part = out_part.reshape(dp_count * ep_count, capacity, feature_count)
    hidden_grad = contract_cols(routed_grad, down_matrix)
    preact_grad = (hidden_grad * silu_grad(preact)).astype(jnp.bfloat16)
    input_part = contract_cols(preact_grad, up_matrix)
    input_part = input_part.reshape(dp_count * ep_count, capacity, feature_count)
    out_sum, input_sum = (
        lax.psum_scatter(
            out_part.astype(jnp.bfloat16), "dp", scatter_dimension=0, tiled=True
        ).astype(jnp.float32),
        lax.psum_scatter(
            input_part.astype(jnp.bfloat16), "dp", scatter_dimension=0, tiled=True
        ).astype(jnp.float32),
    )
    out_back, input_back = (
        lax.all_to_all(out_sum.astype(jnp.bfloat16), "ep", split_axis=0, concat_axis=0, tiled=True),
        lax.all_to_all(
            input_sum.astype(jnp.bfloat16), "ep", split_axis=0, concat_axis=0, tiled=True
        ),
    )
    up_grad = contract_rows(routed, preact_grad).astype(jnp.bfloat16)[None]
    down_grad = contract_rows(hidden, routed_grad).astype(jnp.bfloat16)[None]
    mixed = contract_rows(select, out_back.reshape(slot_count, feature_count))
    outputs = (router_weight[:, None] * mixed).astype(jnp.bfloat16)
    input_grad = contract_rows(select, input_back.reshape(slot_count, feature_count)).astype(
        jnp.bfloat16
    )
    return (outputs, input_grad, up_grad, down_grad)


def solution(mesh):
    in_specs = (
        P(("ep", "dp"), None),
        P(("ep", "dp"), None),
        P(("ep", "dp"), None),
        P(("ep", "dp"), None),
        P("ep", None, "dp"),
        P("ep", "dp", None),
        P(),
    )
    out_specs = (
        P(("ep", "dp"), None),
        P(("ep", "dp"), None),
        P("ep", None, "dp"),
        P("ep", "dp", None),
    )
    return jax.shard_map(shards, mesh=mesh, in_specs=in_specs, out_specs=out_specs, check_vma=False)
```

profile of v0, /device:TPU:1, one launch (start us, length us, event | category | flops | bytes accessed | tf_op | source)
XLA Modules:
  0.0 474.4 jit_solution(4635988429792891235)
XLA Ops:
  10.2 1.6 convolution_convert_fusion.5
  11.8 2.6 reshape.76
  14.4 56.2 %all_to_all.20 = bf16[64,3,3584]{2,1,0:T(4,128)(2,1)S(1)} all-to-all(bf16[64,3,3584]{2,1,0:T(4,128)(2,1)S(1)} %reshape.76), channel_id=1, replica_groups=mesh['ep'=64,'dp'=4] {'ep'}, dimensions={0} | all-to-all | bytes 2752512 | tf_op jit(solution)/shard_map/all_to_all | solution.py:71
  70.6 1.4 copy.25
  72.0 1.7 convolution_convert_fusion.4
  73.7 2.6 reshape.79
  76.3 50.2 %all_to_all.21 = bf16[64,3,3584]{2,1,0:T(4,128)(2,1)S(1)} all-to-all(bf16[64,3,3584]{2,1,0:T(4,128)(2,1)S(1)} %reshape.79), channel_id=1, replica_groups=mesh['ep'=64,'dp'=4] {'ep'}, dimensions={0} | all-to-all | bytes 2752512 | tf_op jit(solution)/shard_map/all_to_all | solution.py:72
  126.5 1.4 copy.29
  127.9 1.3 collective-permute-start
  131.0 11.0 %all-gather.3.cloned.1.call-done = bf16[256,3,3584]{2,0,1:T(8,128)(2,1)} async-done(((bf16[64,3,3584]{2,0,1:T(8,128)(2,1)}), bf16[256,3,3584]{2,0,1:T(8,128)(2,1)}) %all-gather.3.cloned.1.call-update) | async-done | bytes 5505040 | tf_op jit(solution)/shard_map/all_gather | solution.py:75
  142.0 10.2 %copy.26 = bf16[256,3,3584]{2,1,0:T(4,128)(2,1)} copy(bf16[256,3,3584]{2,0,1:T(8,128)(2,1)} %all-gather.3.cloned.1.call-done) | data formatting | bytes 11010048 | tf_op jit(solution)/shard_map/all_gather | solution.py:75
  152.2 13.2 %reshape.77 = bf16[768,3584]{1,0:T(8,128)(2,1)} reshape(bf16[256,3,3584]{2,1,0:T(4,128)(2,1)} %copy.26) | data formatting | bytes 11010048 | tf_op jit(solution)/shard_map/reshape | solution.py:79
  165.4 61.0 %all-gather.5.cloned.1.call-done = bf16[256,3,3584]{2,0,1:T(8,128)(2,1)} async-done(((bf16[64,3,3584]{2,0,1:T(8,128)(2,1)}), bf16[256,3,3584]{2,0,1:T(8,128)(2,1)}) %all-gather.5.cloned.1.call-update) | async-done | bytes 5505040 | tf_op jit(solution)/shard_map/all_gather | solution.py:76
  226.4 10.2 %copy.30 = bf16[256,3,3584]{2,1,0:T(4,128)(2,1)} copy(bf16[256,3,3584]{2,0,1:T(8,128)(2,1)} %all-gather.5.cloned.1.call-done) | data formatting | bytes 11010048 | tf_op jit(solution)/shard_map/all_gather | solution.py:76
  236.6 13.0 %reshape.80 = bf16[768,3584]{1,0:T(8,128)(2,1)} reshape(bf16[256,3,3584]{2,1,0:T(4,128)(2,1)} %copy.30) | data formatting | bytes 11010048 | tf_op jit(solution)/shard_map/reshape | solution.py:80
  249.7 4.9 %multiply_convert_fusion.2 = (bf16[768,256]{1,0:T(8,128)(2,1)S(1)}, f32[768,256]{1,0:T(8,128)S(1)}) fusion(bf16[768,3584]{1,0:T(8,128)(2,1)} %reshape.77, bf16[1,3584,256]{2,1,0:T(8,128)(2,1)} %collective-permute-done, bf16[1,3584,256]{2,1,0:T(8,128)(2,1)} %param.11, pred[]{:T(512)S(6)} %eq.95), kind=kOutput, calls=%fused_computation.23 | convolution fusion | flops 1411186688 | bytes 10354689 | tf_op jit(solution)/shard_map/dot_general | solution.py:81
  254.6 1.7 fusion.12
  256.4 5.6 %convolution_convert_fusion = bf16[256,3,3584]{2,0,1:T(8,128)(2,1)} fusion(bf16[1,3584,256]{2,1,0:T(8,128)(2,1)} %collective-permute-done, bf16[1,3584,256]{2,1,0:T(8,128)(2,1)} %param.11, pred[]{:T(512)S(6)} %eq.95, bf16[256,3,256]{2,1,0:T(4,128)(2,1)S(1)} %dot_general.41), kind=kOutput, calls=%fused_computation | convolution fusion | flops 1412956160 | bytes 9568257 | tf_op jit(solution)/shard_map/dot_general | solution.py:23
  262.5 4.1 convolution_convert_fusion.1
  266.6 61.1 %reduce-scatter.5.cloned.1.call-done = bf16[64,3,3584]{2,0,1:T(8,128)(2,1)} async-done(((bf16[256,3,3584]{2,0,1:T(8,128)(2,1)}), bf16[64,3,3584]{2,0,1:T(8,128)(2,1)}) %reduce-scatter.5.cloned.1.call-update) | async-done | bytes 1376272 | tf_op jit(solution)/shard_map/reduce_scatter | solution.py:93
  327.6 3.7 copy.32
  331.4 10.2 %all-to-all-start.3 = ((bf16[64,3,3584]{2,1,0:T(4,128)(2,1)}), bf16[64,3,3584]{2,1,0:T(4,128)(2,1)S(1)}, u32[]{:S(2)}, u32[]{:S(2)}) async-start(bf16[64,3,3584]{2,1,0:T(4,128)(2,1)} %copy.32), calls=%async_computation.5 | async-start | bytes 3670016 | tf_op jit(solution)/shard_map/all_to_all | solution.py:99
  341.6 64.0 %reduce-scatter.3.cloned.1.call-done = bf16[64,3,3584]{2,0,1:T(8,128)(2,1)} async-done(((bf16[256,3,3584]{2,0,1:T(8,128)(2,1)}), bf16[64,3,3584]{2,0,1:T(8,128)(2,1)}) %reduce-scatter.3.cloned.1.call-update) | async-done | bytes 1376272 | tf_op jit(solution)/shard_map/reduce_scatter | solution.py:90
  405.5 3.8 copy.28
  409.3 10.4 %all-to-all-start.1 = ((bf16[64,3,3584]{2,1,0:T(4,128)(2,1)}), bf16[64,3,3584]{2,1,0:T(4,128)(2,1)}, u32[]{:S(2)}, u32[]{:S(2)}) async-start(bf16[64,3,3584]{2,1,0:T(4,128)(2,1)} %copy.28), calls=%async_computation.2 | async-start | bytes 3670016 | tf_op jit(solution)/shard_map/all_to_all | solution.py:98
  419.7 5.4 %fusion.1 = bf16[1,256,3584]{2,1,0:T(8,128)(2,1)} fusion(bf16[768,256]{1,0:T(8,128)(2,1)S(1)} %get-tuple-element.4, bf16[768,3584]{1,0:T(8,128)(2,1)} %reshape.80), kind=kOutput, calls=%fused_computation.8 | convolution fusion | flops 1410203648 | bytes 7733248 | tf_op jit(solution)/shard_map/dot_general | solution.py:17
  425.1 5.4 %fusion = bf16[1,3584,256]{2,1,0:T(8,128)(2,1)} fusion(bf16[768,3584]{1,0:T(8,128)(2,1)} %reshape.77, bf16[768,256]{1,0:T(8,128)(2,1)S(1)} %fusion.12), kind=kOutput, calls=%fused_computation.7 | convolution fusion | flops 1410203648 | bytes 7733248 | tf_op jit(solution)/shard_map/dot_general | solution.py:17
  430.6 2.4 reshape.81
  432.9 2.7 convolution_convert_fusion.6
  435.6 27.7 %all-to-all-done.1 = bf16[64,3,3584]{2,1,0:T(4,128)(2,1)} async-done(((bf16[64,3,3584]{2,1,0:T(4,128)(2,1)}), bf16[64,3,3584]{2,1,0:T(4,128)(2,1)}, u32[]{:S(2)}, u32[]{:S(2)}) %all-to-all-start.1) | async-done | bytes 1376288 | tf_op jit(solution)/shard_map/all_to_all | solution.py:98
  463.4 3.0 reshape.78
  466.4 1.4 fusion.2
  (35 shorter events, 4.9 us)
Async XLA Ops:
  7.2 3.1 copy-start
  7.2 134.8 %all-gather.3.cloned.1.call-start = ((), (), s32[]{:S(2)}) async-start(), calls=%async_computation.6 | async-start | bytes 6881280 | tf_op jit(solution)/shard_map/all_gather | solution.py:75
  70.5 1.4 copy-start.4
  70.6 1.5 copy-start.5
  71.9 154.4 %all-gather.5.cloned.1.call-start = ((), (), s32[]{:S(2)}) async-start(), calls=%async_computation.8 | async-start | bytes 6881280 | tf_op jit(solution)/shard_map/all_gather | solution.py:76
  126.5 2.7 copy-start.3
  126.5 3.2 copy-start.6
  127.9 199.7 %reduce-scatter.5.cloned.1.call-start = ((), (), s32[]{:S(2)}) async-start(), calls=%async_computation.9 | async-start | bytes 6881280 | tf_op jit(solution)/shard_map/reduce_scatter | solution.py:93
  127.9 121.7 %collective-permute-start = (bf16[1,3584,256]{2,1,0:T(8,128)(2,1)}, bf16[1,3584,256]{2,1,0:T(8,128)(2,1)}, u32[]{:S(2)}, u32[]{:S(2)}) collective-permute-start(bf16[1,3584,256]{2,1,0:T(8,128)(2,1)} %param.11), channel_id=1, source_target_pairs={{0,128},{4,132},{8,136},{12,140},{16,144},{20,148},{24,152},{28,15... | collective-permute-start | bytes 5505032 | tf_op jit(solution)/shard_map/ppermute | solution.py:8
  129.2 125.3 %collective-permute-start.1 = (bf16[1,256,3584]{2,1,0:T(8,128)(2,1)S(1)}, bf16[1,256,3584]{2,1,0:T(8,128)(2,1)}, u32[]{:S(2)}, u32[]{:S(2)}) collective-permute-start(bf16[1,256,3584]{2,1,0:T(8,128)(2,1)S(1)} %copy-done.3), channel_id=1, source_target_pairs={{0,128},{4,132},{8,136},{12,140},{16,144},{20,148},{24,152},{28,15... | collective-permute-start | bytes 5505032 | tf_op jit(solution)/shard_map/ppermute | solution.py:8
  249.7 4.9 %copy-start.2 = (bf16[768,3584]{1,0:T(8,128)(2,1)S(1)}, bf16[768,3584]{1,0:T(8,128)(2,1)}, u32[]{:S(2)}) copy-start(bf16[768,3584]{1,0:T(8,128)(2,1)} %reshape.80) | copy-start | bytes 16515076
  262.0 143.5 %reduce-scatter.3.cloned.1.call-start = ((), (), s32[]{:S(2)}) async-start(), calls=%async_computation.7 | async-start | bytes 6881280 | tf_op jit(solution)/shard_map/reduce_scatter | solution.py:90
  331.4 78.0 %all-to-all-start.3 = ((bf16[64,3,3584]{2,1,0:T(4,128)(2,1)}), bf16[64,3,3584]{2,1,0:T(4,128)(2,1)S(1)}, u32[]{:S(2)}, u32[]{:S(2)}) async-start(bf16[64,3,3584]{2,1,0:T(4,128)(2,1)} %copy.32), calls=%async_computation.5 | async-start | bytes 3670016 | tf_op jit(solution)/shard_map/all_to_all | solution.py:99
  409.3 54.1 %all-to-all-start.1 = ((bf16[64,3,3584]{2,1,0:T(4,128)(2,1)}), bf16[64,3,3584]{2,1,0:T(4,128)(2,1)}, u32[]{:S(2)}, u32[]{:S(2)}) async-start(bf16[64,3,3584]{2,1,0:T(4,128)(2,1)} %copy.28), calls=%async_computation.2 | async-start | bytes 3670016 | tf_op jit(solution)/shard_map/all_to_all | solution.py:98
  463.4 4.4 copy-start.1
Sparse Core Ops, SparseCore 0:
  72.1 69.8 all-gather.2
  144.4 81.9 all-gather.4
  262.1 65.4 reduce-scatter.4
  330.5 75.0 reduce-scatter.2
where the time goes:
time: 478 us; the launch traced here: 474 us
  waiting for transfers between devices  225 us (47%)
  blocking collectives  106 us (22%)
  local copies, waits for them, and re-layouts  67.8 us (14%)
  matrix products  34.4 us (7%)
  starting transfers between devices  22.7 us (5%)
  between operations  14.6 us (3%)
    reduce_scatter x1, waiting for transfers between devices, shards(): lax.psum_scatter(out_part.astype(jnp.bfloat16), 'dp', scatter_dimension=0...  64 us
    reduce_scatter x1, waiting for transfers between devices, shards(): lax.psum_scatter(input_part.astype(jnp.bfloat16), 'dp', scatter_dimension...  61.1 us
    all_gather x1, waiting for transfers between devices, shards(): lax.all_gather(arrived_grad, 'dp', axis=0, tiled=True)  61 us
    all_to_all x1, blocking collectives, shards(): lax.all_to_all(token_buffer, 'ep', split_axis=0, concat_axis=0, tiled=True)  56.2 us
    all_to_all x1, blocking collectives, shards(): lax.all_to_all(grad_buffer, 'ep', split_axis=0, concat_axis=0, tiled=True)  50.2 us
    all_to_all x1, waiting for transfers between devices, shards(): lax.all_to_all(out_sum.astype(jnp.bfloat16), 'ep', split_axis=0, concat_a...  27.7 us
    dot_general x4, matrix products, contract_rows(): lax.dot_general(left, right, (((0,), (0,)), ((), ())), preferred_element_...  14.9 us
    reshape x1, local copies, waits for them, and re-layouts, shards(): routed = routed.reshape(row_count, feature_count)  13.2 us
  transfers between devices with their start and end apart: 8, of which 5 were waited for; matrix products, arithmetic and copies ran while one was open for 18% of the time, Pallas kernels for 0%

commit v1 on v0

v1 whole, which is shorter than its diff:
```python
import functools

import jax
import jax.numpy as jnp
import numpy as np
from jax import lax
from jax.experimental import pallas as pl
from jax.experimental.pallas import tpu as pltpu
from jax.sharding import PartitionSpec as P

MESH = pl.DeviceIdType.MESH
NX = 4
CAP = 3
BF16 = jnp.bfloat16
F32 = jnp.float32


def dot(left, right, dims=((1,), (0,))):
    return lax.dot_general(left, right, (dims, ((), ())), preferred_element_type=F32)


def columns(width, parts, body):
    step = width // parts

    def run(i, _):
        body(pl.ds(pl.multiple_of(i * step, step), step))
        return 0

    lax.fori_loop(0, parts, run, 0)


class Geometry:
    def __init__(self, ny, nz):
        self.ny, self.nz = ny, nz
        self.zrows = 2 * ny * 2 * CAP
        self.yrows = 2 * nz * CAP
        self.xrows = ny * nz * CAP
        self.rows = 2 * self.xrows

    def matrices(self):
        ny, nz, rows = self.ny, self.nz, self.rows
        by_z = np.arange(rows).reshape(nz, ny, 2, CAP)
        by_y = by_z.transpose(1, 2, 0, 3).reshape(-1)
        per_z = ny * 2 * CAP
        split = lambda source, h: (source // per_z) * 2 * per_z + h * per_z + source % per_z
        to_y = np.zeros((2, rows, 2 * rows), np.float32)
        for h in range(2):
            to_y[h, np.arange(rows), split(by_y, h)] = 1
        at_y = np.arange(rows).reshape(ny, 2, nz, CAP)
        by_r = at_y.transpose(1, 0, 2, 3).reshape(-1)
        to_x = np.zeros((rows, rows), np.float32)
        to_x[np.arange(rows), by_r] = 1
        return [
            m.astype(jnp.bfloat16)
            for m in (to_y, to_y.transpose(0, 2, 1), to_x, to_x.T)
        ]


def kernel(
    geo,
    tokens,
    cotangent,
    weight,
    select,
    unselect,
    to_y,
    from_y,
    to_x,
    from_x,
    flag,
    up_own,
    down_own,
    outputs,
    input_grad,
    up_grad,
    down_grad,
    up,
    down,
    preact,
    hidden,
    slope,
    sent,
    got_z,
    got_y,
    routed,
    part,
    core_part,
    x_part,
    back_y,
    back_z,
    send_sem,
    recv_sem,
    out_sem,
):
    ny, nz = geo.ny, geo.nz
    xr, yr, zr, rows = geo.xrows, geo.yrows, geo.zrows, geo.rows
    width = tokens.shape[1]
    half = width // 2
    ep, dp = lax.axis_index("ep"), lax.axis_index("dp")
    x_lo, y, z = ep // (ny * nz), (ep // nz) % ny, ep % nz
    x, core = (dp // 2) * 2 + x_lo, dp % 2

    def at(dx=0, dy=0, dz=0, dc=0):
        nx_, ny_, nz_ = (x + dx) % NX, (y + dy % ny) % ny, (z + dz % nz) % nz
        return ((nx_ % 2) * (ny * nz) + ny_ * nz + nz_, (nx_ // 2) * 2 + (core + dc) % 2)

    used = {}

    def remote(key, src, dst, device):
        number = used.setdefault(key, len(used))
        return pltpu.make_async_remote_copy(
            src_ref=src,
            dst_ref=dst,
            send_sem=send_sem.at[number],
            recv_sem=recv_sem.at[number],
            device_id=device,
            device_id_type=MESH,
        )

    peers = (
        [at(dz=d) for d in range(1, nz)]
        + [at(dy=d) for d in range(1, ny)]
        + [at(dx=d) for d in range(1, NX)]
        + [at(dc=1)]
    )
    barrier = pltpu.get_barrier_semaphore()
    for peer in peers:
        pl.semaphore_signal(barrier, inc=1, device_id=peer, device_id_type=MESH)
    pl.semaphore_wait(barrier, len(peers))

    waiting = {}

    def start(copy):
        copy.start()
        waiting[id(copy)] = copy
        return copy

    def settle(copies):
        for copy in copies:
            copy.wait_send()
            del waiting[id(copy)]

    def z_block(d):
        return pl.ds(d * zr, zr)

    def y_block(d):
        return pl.ds(d * yr, yr)

    def x_block(d):
        return pl.ds(d * xr, xr)

    def pick(s):
        def tile(cols):
            far = pl.ds(cols.start + half, cols.size)
            if s == 0:
                near_part, far_part = tokens[:, cols], tokens[:, far]
            else:
                near_part = (weight[...] * cotangent[:, cols].astype(F32)).astype(BF16)
                far_part = (weight[...] * cotangent[:, far].astype(F32)).astype(BF16)
            both = jnp.concatenate([near_part, far_part], axis=0)
            sent[s, :, cols] = dot(select[...], both).astype(BF16)

        columns(half, 7, tile)
        got_z[s, z_block(0), :] = sent[s, z_block(0), :]
        return [
            start(remote(("z", s, d), sent.at[s, z_block(d)], got_z.at[s, z_block(d)], at(dz=d)))
            for d in range(1, nz)
        ]

    def to_ring_y(s, copies):
        for copy in copies:
            copy.wait_recv()

        def tile(cols):
            block = got_z[s, :, cols]
            far = pl.ds(cols.start + half, cols.size)
            part[s, pl.ds(0, rows), cols] = dot(to_y[0], block).astype(BF16)
            part[s, pl.ds(0, rows), far] = dot(to_y[1], block).astype(BF16)

        columns(half, 7, tile)
        got_y[s, y_block(0), :] = part[s, y_block(0), :]
        return [
            start(remote(("y", s, d), part.at[s, y_block(d)], got_y.at[s, y_block(d)], at(dy=d)))
            for d in range(1, ny)
        ]

    def to_ring_x(s, copies):
        for copy in copies:
            copy.wait_recv()

        def tile(cols):
            block = dot(to_x[...], got_y[s, :, cols]).astype(BF16)
            routed[s, x_block(0), cols] = block[:xr]
            part[s, pl.ds(rows, xr), cols] = block[xr:]

        columns(width, 7, tile)
        other = part.at[s, pl.ds(rows, xr)]
        own = routed.at[s, x_block(0)]
        made = {
            1: start(remote(("x", s, 1), other, routed.at[s, x_block(2)], at(dx=1))),
            3: start(remote(("x", s, 3), other, routed.at[s, x_block(6)], at(dx=3))),
            2: start(remote(("x", s, 2), own, routed.at[s, x_block(4)], at(dx=2))),
            0: start(remote(("c", s, 0), own, routed.at[s, x_block(1)], at(dc=1))),
        }
        return made

    def share(s, made):
        shared = {0: made[0]}
        for d in (1, 3, 2):
            made[d].wait_recv()
            block = routed.at[s, x_block(2 * d)]
            shared[d] = start(
                remote(("c", s, d), block, routed.at[s, x_block(2 * d + 1)], at(dc=1))
            )
        return shared

    def take_weights(swaps):
        chosen = flag[0] == 1
        for copy, buffer, own, parts in zip(swaps, (up, down), (up_own, down_own), (7, 4)):
            copy.wait_recv()
            step = buffer.shape[0] // parts

            def run(i, _, buffer=buffer, own=own, step=step):
                at_rows = pl.ds(pl.multiple_of(i * step, step), step)
                buffer[at_rows, :] = lax.select(chosen, buffer[at_rows, :], own[at_rows, :])
                return 0

            lax.fori_loop(0, parts, run, 0)

    def send_core(s, d):
        return start(
            remote(
                ("p", s, d), part.at[s, x_block(2 * d + 1)], core_part.at[s, x_block(d)], at(dc=1)
            )
        )

    def forward(shared):
        made = {}
        for d in (0, 1, 3, 2):
            shared[d].wait_recv()
            pair = pl.ds(2 * d * xr, 2 * xr)
            value = dot(routed[0, pair, :], up[...])
            sigmoid = jax.nn.sigmoid(value)
            active = (value * sigmoid).astype(BF16)
            slope[pair, :] = sigmoid * (1.0 + value * (1.0 - sigmoid))
            hidden[pair, :] = active

            def tile(cols, active=active, pair=pair):
                part[0, pair, cols] = dot(active, down[:, cols]).astype(BF16)

            columns(width, 7, tile)
            made[d] = send_core(0, d)
        return made

    def backward(shared):
        made = {}
        for d in (0, 1, 3, 2):
            shared[d].wait_recv()
            pair = pl.ds(2 * d * xr, 2 * xr)
            value = dot(routed[1, pair, :], down[...], ((1,), (1,)))
            grad = (value * slope[pair, :]).astype(BF16)
            preact[pair, :] = grad

            def tile(i, _, grad=grad, pair=pair):
                step = width // 7
                cols = pl.ds(pl.multiple_of(i * step, step), step)
                part[1, pair, cols] = dot(grad, up[cols, :], ((1,), (1,))).astype(BF16)
                return 0

            lax.fori_loop(0, 7, tile, 0)
            made[d] = send_core(1, d)
        return made

    def add_into(target, s, first, other, second):
        def tile(cols):
            total = target[s, first, cols].astype(F32) + other[s, second, cols].astype(F32)
            target[s, first, cols] = total.astype(BF16)

        columns(width, 7, tile)

    def chip_sums(s, made):
        back = {}
        for d, place in ((1, 1), (3, 2), (2, 0), (0, None)):
            made[d].wait_recv()
            add_into(part, s, x_block(2 * d), core_part, x_block(d))
            if d:
                back[d] = start(
                    remote(
                        ("b", s, d),
                        part.at[s, x_block(2 * d)],
                        x_part.at[s, x_block(place)],
                        at(dx=NX - d),
                    )
                )
        return back

    def from_ring_x(s, back):
        for d in (1, 3, 2):
            back[d].wait_recv()

        def tile(cols):
            same = part[s, x_block(0), cols].astype(F32) + x_part[s, x_block(0), cols].astype(F32)
            cross = x_part[s, x_block(1), cols].astype(F32) + x_part[s, x_block(2), cols].astype(F32)
            both = jnp.concatenate([same.astype(BF16), cross.astype(BF16)], axis=0)
            got_y[s, :, cols] = dot(from_x[...], both).astype(BF16)

        columns(width, 7, tile)
        back_y[s, y_block(0), :] = got_y[s, y_block(0), :]
        return [
            start(remote(("v", s, d), got_y.at[s, y_block(d)], back_y.at[s, y_block(d)], at(dy=-d)))
            for d in range(1, ny)
        ]

    def from_ring_y(s, copies, dispatched):
        for copy in copies:
            copy.wait_recv()
        settle(dispatched)

        def tile(cols):
            far = pl.ds(cols.start + half, cols.size)
            near_rows = dot(from_y[0], back_y[s, :, cols])
            far_rows = dot(from_y[1], back_y[s, :, far])
            sent[s, :, cols] = (near_rows + far_rows).astype(BF16)

        columns(half, 7, tile)
        back_z[s, z_block(0), :] = sent[s, z_block(0), :]
        return [
            start(remote(("w", s, d), sent.at[s, z_block(d)], back_z.at[s, z_block(d)], at(dz=-d)))
            for d in range(1, nz)
        ]

    def finish(s, copies, out):
        for copy in copies:
            copy.wait_recv()
        count = tokens.shape[0]

        def tile(cols):
            for h in range(2):
                place = pl.ds(cols.start + h * half, cols.size)
                picked = dot(unselect[pl.ds(h * count, count), :], back_z[s, :, cols])
                out[:, place] = (picked if s else weight[...] * picked).astype(BF16)

        columns(half, 7, tile)

    z_t = pick(0)
    swaps = [
        start(remote(("s", i), own, buffer, at(dx=1 + 2 * x_lo)))
        for i, (own, buffer) in enumerate(((up_own, up), (down_own, down)))
    ]
    z_g = pick(1)
    y_t = to_ring_y(0, z_t)
    x_t = to_ring_x(0, y_t)
    y_g = to_ring_y(1, z_g)
    shared_t = share(0, x_t)
    x_g = to_ring_x(1, y_g)
    take_weights(swaps)
    settle(y_t + [x_t[1], x_t[3]])
    made_t = forward(shared_t)
    shared_g = share(1, x_g)
    back_t = chip_sums(0, made_t)
    settle(y_g + [x_g[1], x_g[3]])
    made_g = backward(shared_g)
    v_t = from_ring_x(0, back_t)
    back_g = chip_sums(1, made_g)
    w_t = from_ring_y(0, v_t, z_t)

    def up_tile(i, _):
        step = width // 7
        cols = pl.ds(pl.multiple_of(i * step, step), step)
        up[cols, :] = dot(routed[0, :, cols], preact[...], ((0,), (0,))).astype(BF16)
        return 0

    lax.fori_loop(0, 7, up_tile, 0)
    write_up = pltpu.make_async_copy(up, up_grad, out_sem.at[0])
    write_up.start()
    v_g = from_ring_x(1, back_g)
    w_g = from_ring_y(1, v_g, z_g)

    def down_tile(cols):
        down[:, cols] = dot(hidden[...], routed[1, :, cols], ((0,), (0,))).astype(BF16)

    columns(width, 7, down_tile)
    write_down = pltpu.make_async_copy(down, down_grad, out_sem.at[1])
    write_down.start()
    finish(0, w_t, outputs)
    finish(1, w_g, input_grad)
    settle(list(waiting.values()))
    write_up.wait()
    write_down.wait()


def shards(geo, tokens, cotangent, routes, router_probs, up_weight, down_weight, moving):
    ny, nz = geo.ny, geo.nz
    count, width = tokens.shape
    hid = up_weight.shape[2]
    half_count = ny * nz
    rows, xr = geo.rows, geo.xrows
    ep_index = lax.axis_index("ep")
    pair_ids = jnp.arange(half_count, dtype=jnp.int32)
    swapped = jnp.sum(jnp.where(pair_ids == ep_index % half_count, moving, 0), keepdims=True)
    expert_of = routes[:, 0]
    flip = jnp.sum(
        jnp.where((expert_of % half_count)[:, None] == pair_ids[None, :], moving[None, :], 0), axis=1
    )
    target = (expert_of + half_count * flip) % (2 * half_count)
    order = jnp.arange(count, dtype=jnp.int32)
    rank = jnp.sum(
        ((target[:, None] == target[None, :]) & (order[None, :] < order[:, None])).astype(jnp.int32),
        axis=1,
    )
    dz = (target % nz - ep_index % nz + nz) % nz
    dy = (target // nz % ny - ep_index // nz % ny + ny) % ny
    cross = (target // half_count + ep_index // half_count) % 2
    near = dz * geo.zrows + (dy * 2 + cross) * CAP + rank
    slot = jnp.concatenate([near, near + geo.zrows // 2])
    place = jnp.arange(2 * rows, dtype=jnp.int32)
    select = (place[:, None] == slot[None, :]).astype(BF16)
    unselect = (slot[:, None] == place[None, :]).astype(BF16)
    vmem = pl.BlockSpec(memory_space=pltpu.VMEM)
    copies = 2 * (2 * (nz - 1) + 2 * (ny - 1) + 3 + 4 + 4 + 3) + 2
    buffer = lambda *shape: pltpu.VMEM(shape, BF16)
    outputs, input_grad, up_grad, down_grad = pl.pallas_call(
        functools.partial(kernel, geo),
        out_shape=(
            jax.ShapeDtypeStruct((count, width), BF16),
            jax.ShapeDtypeStruct((count, width), BF16),
            jax.ShapeDtypeStruct((width, hid), BF16),
            jax.ShapeDtypeStruct((hid, width), BF16),
        ),
        in_specs=[vmem] * 9 + [pl.BlockSpec(memory_space=pltpu.SMEM)] + [vmem] * 2,
        out_specs=(vmem, vmem) + (pl.BlockSpec(memory_space=pl.ANY),) * 2,
        scratch_shapes=[
            buffer(width, hid),
            buffer(hid, width),
            buffer(8 * xr, hid),
            buffer(8 * xr, hid),
            pltpu.VMEM((8 * xr, hid), F32),
            buffer(2, 2 * rows, width // 2),
            buffer(2, 2 * rows, width // 2),
            buffer(2, rows, width),
            buffer(2, 8 * xr, width),
            buffer(2, 8 * xr, width),
            buffer(2, 4 * xr, width),
            buffer(2, 3 * xr, width),
            buffer(2, rows, width),
            buffer(2, 2 * rows, width // 2),
            pltpu.SemaphoreType.DMA((copies,)),
            pltpu.SemaphoreType.DMA((copies,)),
            pltpu.SemaphoreType.DMA((2,)),
        ],
        compiler_params=pltpu.CompilerParams(
            collective_id=0, has_side_effects=True, vmem_limit_bytes=63 * 2**20
        ),
    )(
        tokens,
        cotangent,
        router_probs,
        select,
        unselect,
        *[jnp.asarray(m) for m in geo.matrices()],
        swapped,
        up_weight[0],
        down_weight[0],
    )
    return outputs, input_grad, up_grad[None], down_grad[None]


def solution(mesh):
    ep_count = mesh.shape["ep"]
    nz = 8 if ep_count == 64 else 2
    geo = Geometry(ep_count // 2 // nz, nz)
    in_specs = (
        P(("ep", "dp"), None),
        P(("ep", "dp"), None),
        P(("ep", "dp"), None),
        P(("ep", "dp"), None),
        P("ep", None, "dp"),
        P("ep", "dp", None),
        P(),
    )
    out_specs = (
        P(("ep", "dp"), None),
        P(("ep", "dp"), None),
        P("ep", None, "dp"),
        P("ep", "dp", None),
    )
    return jax.shard_map(
        functools.partial(shards, geo),
        mesh=mesh,
        in_specs=in_specs,
        out_specs=out_specs,
        check_vma=False,
    )
```

time: 478 us -> 288 us (0.60)
  Pallas kernels: 0 us -> 274 us
  waiting for transfers between devices: 225 us -> 0 us
  blocking collectives: 106 us -> 0 us
  local copies, waits for them, and re-layouts: 67.8 us -> 8.02 us
  matrix products: 34.4 us -> 0 us
  starting transfers between devices: 22.7 us -> 0 us
  between operations: 14.6 us -> 0.73 us
    pallas_call x0 -> x1, Pallas kernels: none -> 274 us  [shards(): pl.pallas_call(functools.partial(kernel, geo), out_shape=(jax.ShapeDtypeS...]
    reduce_scatter x2 -> x0, waiting for transfers between devices: 125 us -> none  [the longest x1 64 us: shards(): lax.psum_scatter(out_part.astype(jnp.bfloat16), 'dp', scatter_dimension=0...]
    all_to_all x2 -> x0, blocking collectives: 106 us -> none  [the longest x1 56.2 us: shards(): lax.all_to_all(token_buffer, 'ep', split_axis=0, concat_axis=0, tiled=True)]
    all_gather x2 -> x0, waiting for transfers between devices: 72 us -> none  [the longest x1 61 us: shards(): lax.all_gather(arrived_grad, 'dp', axis=0, tiled=True)]
    reshape x6 -> x0, local copies, waits for them, and re-layouts: 36.7 us -> none  [the longest x1 13.2 us: shards(): routed = routed.reshape(row_count, feature_count)]
    dot_general x10 -> x0, matrix products: 34.4 us -> none  [the longest x4 14.9 us: contract_rows(): lax.dot_general(left, right, (((0,), (0,)), ((), ())), preferred_element_...]
    all_to_all x2 -> x0, waiting for transfers between devices: 27.7 us -> none  [the longest x1 27.7 us: shards(): lax.all_to_all(out_sum.astype(jnp.bfloat16), 'ep', split_axis=0, concat_a...]
    all_to_all x2 -> x0, starting transfers between devices: 20.6 us -> none  [the longest x1 10.4 us: shards(): lax.all_to_all(out_sum.astype(jnp.bfloat16), 'ep', split_axis=0, concat_a...]
  transfers between devices with their start and end apart: 8 -> 0, of which waited for: 5 -> 0; matrix products, arithmetic and copies ran while one was open for 18% -> 0% of each run, Pallas kernels for 0% -> 0%
where the time goes in v1:
time: 288 us
  Pallas kernels  274 us (95%)
  local copies, waits for them, and re-layouts  8.02 us (3%)
  other arithmetic  5.75 us (2%)
    pallas_call x1, Pallas kernels, shards(): pl.pallas_call(functools.partial(kernel, geo), out_shape=(jax.ShapeDtypeS...  274 us
    unnamed x11, local copies, waits for them, and re-layouts  8.02 us

profile of v1, /device:TPU:1, one launch (start us, length us, event | category | flops | bytes accessed | tf_op | source)
XLA Modules:
  0.0 288.3 jit_solution(16190854393343313790)
XLA Ops:
  0.7 1.3 fusion.14
  2.0 0.7 fusion.4
  2.6 0.7 select_reduce_fusion
  3.4 0.7 and_select_fusion.8
  4.0 0.7 fusion.13
  4.7 0.2 convert_reduce_fusion
  4.9 1.4 copy.16.weight
  6.3 0.8 fusion.1.unselect
  7.1 0.7 fusion.select
  7.8 273.8 %shard_map.138 = (bf16[128,3584]{1,0:T(8,128)(2,1)}, bf16[128,3584]{1,0:T(8,128)(2,1)}, bf16[3584,256]{1,0:T(8,128)(2,1)}, bf16[256,3584]{1,0:T(8,128)(2,1)}) custom-call(bf16[128,3584]{1,0:T(8,128)(2,1)} %tokens.1, bf16[128,3584]{1,0:T(8,128)(2,1)} %cotangent.1, f32[128,1]{1,0:T(8,128)} %copy.16.weight, bf16[384,256]{1,0:T(8,128)(2,1)} %fusion.select, ...), custom_call_target="tpu_custom_call" | custom-call | tf_op jit(solution)/shard_map/pallas_call | solution.py:422
  281.6 0.0 copy-start.2
  281.7 0.0 copy-start.1
  281.7 2.3 copy.21
  284.0 0.0 copy-done.2
  284.0 0.9 copy.22
  284.9 0.0 copy-done.1
  284.9 0.0 copy-start
  284.9 1.2 copy.23
  286.1 0.9 copy-done
  287.1 1.2 copy.24
  (2 shorter events, 0.0 us)
Async XLA Ops:
  281.6 2.3 copy-start.2
  281.7 3.2 %copy-start.1 = (bf16[3584,256]{1,0:T(8,128)(2,1)S(1)}, bf16[3584,256]{1,0:T(8,128)(2,1)}, u32[]{:S(2)}) copy-start(bf16[3584,256]{1,0:T(8,128)(2,1)} %get-tuple-element.10) | copy-start | bytes 5505028
  284.9 2.2 copy-start

commit v2 on v1

v2 whole, which is shorter than its diff:
```python
import functools

import jax
import jax.numpy as jnp
import numpy as np
from jax import lax
from jax.experimental import pallas as pl
from jax.experimental.pallas import tpu as pltpu
from jax.sharding import PartitionSpec as P

MESH = pl.DeviceIdType.MESH
NX = 4
CAP = 3
CHUNKS = 4
BF16 = jnp.bfloat16
F32 = jnp.float32
I32 = jnp.int32


def dot(left, right, dims=((1,), (0,))):
    return lax.dot_general(left, right, (dims, ((), ())), preferred_element_type=F32)


def loop(count, body):
    def run(i, _):
        body(i)
        return 0

    lax.fori_loop(0, count, run, 0)


class Geometry:
    def __init__(self, ny, nz):
        self.ny, self.nz = ny, nz
        self.zrows = ny * 2 * CAP
        self.yrows = 2 * nz * CAP
        self.xrows = ny * nz * CAP
        self.rows = 2 * self.xrows

    def matrices(self):
        ny, nz, rows = self.ny, self.nz, self.rows
        by_z = np.arange(rows).reshape(nz, ny, 2, CAP)
        by_y = np.arange(rows).reshape(ny, 2, nz, CAP)
        to_y = np.zeros((rows, rows), np.float32)
        to_y[np.arange(rows), by_z.transpose(1, 2, 0, 3).reshape(-1)] = 1
        to_x = np.zeros((rows, rows), np.float32)
        to_x[np.arange(rows), by_y.transpose(1, 0, 2, 3).reshape(-1)] = 1
        return [m.astype(jnp.bfloat16) for m in (to_y, to_y.T, to_x, to_x.T)]


def kernel(
    geo,
    tokens_in,
    cotangent_in,
    routes,
    probs,
    moving,
    up_in,
    down_in,
    to_y,
    from_y,
    to_x,
    from_x,
    outputs,
    input_grad,
    up_grad,
    down_grad,
    tokens,
    cotangent,
    up_own,
    down_own,
    up,
    down,
    hidden_grad,
    hidden,
    slope,
    select,
    unselect,
    sent,
    got_z,
    got_y,
    routed,
    part,
    core_part,
    x_part,
    back_y,
    back_z,
    send_sem,
    recv_sem,
    local_sem,
):
    ny, nz = geo.ny, geo.nz
    xr, yr, zr, rows = geo.xrows, geo.yrows, geo.zrows, geo.rows
    count, width = tokens.shape
    wide = width // CHUNKS
    ep, dp = lax.axis_index("ep"), lax.axis_index("dp")
    x_lo, y, z = ep // (ny * nz), (ep // nz) % ny, ep % nz
    x, core = (dp // 2) * 2 + x_lo, dp % 2

    def at(dx=0, dy=0, dz=0, dc=0):
        nx_, ny_, nz_ = (x + dx) % NX, (y + dy % ny) % ny, (z + dz % nz) % nz
        return ((nx_ % 2) * (ny * nz) + ny_ * nz + nz_, (nx_ // 2) * 2 + (core + dc) % 2)

    peers = (
        [at(dz=d) for d in range(1, nz)]
        + [at(dy=d) for d in range(1, ny)]
        + [at(dx=d) for d in range(1, NX)]
        + [at(dc=1)]
    )
    barrier = pltpu.get_barrier_semaphore()
    for peer in peers:
        pl.semaphore_signal(barrier, inc=1, device_id=peer, device_id_type=MESH)

    loads = [
        pltpu.make_async_copy(src, dst, local_sem.at[i])
        for i, (src, dst) in enumerate(
            (
                (tokens_in, tokens),
                (cotangent_in, cotangent),
                (up_in, up_own),
                (down_in, down_own),
            )
        )
    ]
    for load in loads:
        load.start()

    used = {}
    waiting = {}

    def start(key, src, dst, device):
        number = used.setdefault(key, len(used))
        copy = pltpu.make_async_remote_copy(
            src_ref=src,
            dst_ref=dst,
            send_sem=send_sem.at[number],
            recv_sem=recv_sem.at[number],
            device_id=device,
            device_id_type=MESH,
        )
        copy.start()
        waiting[id(copy)] = copy
        return copy

    def settle(copies):
        for copy in copies:
            copy.wait_send()
            del waiting[id(copy)]

    def y_block(d):
        return pl.ds(d * yr, yr)

    def x_block(d):
        return pl.ds(d * xr, xr)

    def chunk_cols(ch):
        return pl.ds(pl.multiple_of(ch * wide, wide), wide)

    half_count = ny * nz
    expert = routes[...]
    flip = jnp.zeros_like(expert)
    for pair in range(half_count):
        flip += jnp.where((expert & (half_count - 1)) == pair, moving[pair], 0)
    target_row = (expert + half_count * flip) & (2 * half_count - 1)
    down_iota = lax.broadcasted_iota(I32, (count, count), 0)
    across_iota = lax.broadcasted_iota(I32, (count, count), 1)

    def as_column(row):
        spread = jnp.where(down_iota == across_iota, row.astype(F32), 0.0)
        return jnp.sum(spread, axis=1, keepdims=True)

    target_column = as_column(target_row).astype(I32)
    same = target_column == target_row
    rank_row = jnp.sum(
        jnp.where(same & (down_iota < across_iota), 1.0, 0.0), axis=0, keepdims=True
    ).astype(I32)

    def slot_of(target, rank):
        dz = (target - z) & (nz - 1)
        dy = (target // nz - y) & (ny - 1)
        cross = (target // half_count) ^ x_lo
        return dz * zr + (dy * 2 + cross) * CAP + rank

    slot_row = slot_of(target_row, rank_row)
    slot_column = as_column(slot_row).astype(I32)
    select[...] = jnp.where(
        lax.broadcasted_iota(I32, (rows, count), 0) == slot_row, 1.0, 0.0
    ).astype(BF16)
    unselect[...] = jnp.where(
        lax.broadcasted_iota(I32, (count, rows), 1) == slot_column, 1.0, 0.0
    ).astype(BF16)
    weight = as_column(probs[...])

    def pick(s):
        loads[s].wait()

        def tile(ch):
            cols = chunk_cols(ch)
            if s == 0:
                given = tokens[:, cols]
            else:
                given = (weight * cotangent[:, cols].astype(F32)).astype(BF16)
            block = dot(select[...], given).astype(BF16)
            for d in range(nz):
                sent[s, ch, d] = block[d * zr : (d + 1) * zr]
            got_z[s, ch, 0] = block[:zr]

        loop(CHUNKS, tile)

    def send_z(s):
        return [
            start(("z", s, d), sent.at[s, :, d], got_z.at[s, :, d], at(dz=d)) for d in range(1, nz)
        ]

    def to_ring_y(s, copies):
        for copy in copies:
            copy.wait_recv()

        def tile(ch):
            block = jnp.concatenate([got_z[s, ch, d] for d in range(nz)], axis=0)
            block = dot(to_y[...], block).astype(BF16)
            part[s, ch, pl.ds(0, rows), :] = block
            got_y[s, ch, y_block(0), :] = block[:yr]

        loop(CHUNKS, tile)
        return [
            start(
                ("y", s, d), part.at[s, :, y_block(d)], got_y.at[s, :, y_block(d)], at(dy=d)
            )
            for d in range(1, ny)
        ]

    def to_ring_x(s, copies):
        for copy in copies:
            copy.wait_recv()

        def tile(ch):
            block = dot(to_x[...], got_y[s, ch]).astype(BF16)
            routed[s, ch, x_block(0), :] = block[:xr]
            part[s, ch, pl.ds(rows, xr), :] = block[xr:]

        loop(CHUNKS, tile)

    def send_x(s):
        other = part.at[s, :, pl.ds(rows, xr)]
        own = routed.at[s, :, x_block(0)]
        return {
            1: start(("x", s, 1), other, routed.at[s, :, x_block(1)], at(dx=1)),
            3: start(("x", s, 3), other, routed.at[s, :, x_block(3)], at(dx=3)),
            2: start(("x", s, 2), own, routed.at[s, :, x_block(2)], at(dx=2)),
            0: start(("c", s, 0), own, routed.at[s, :, x_block(4)], at(dc=1)),
        }

    def share(s, made):
        shared = [made[0]]
        for d in (1, 3, 2):
            made[d].wait_recv()
            shared.append(
                start(
                    ("c", s, d),
                    routed.at[s, :, x_block(d)],
                    routed.at[s, :, x_block(4 + d)],
                    at(dc=1),
                )
            )
        return shared

    def take_weights(swaps):
        chosen = moving[ep % half_count] == 1
        for copy, load, buffer, own, parts in zip(
            swaps, loads[2:], (up, down), (up_own, down_own), (7, 4)
        ):
            load.wait()
            copy.wait_recv()
            step = buffer.shape[0] // parts

            def run(i, buffer=buffer, own=own, step=step):
                at_rows = pl.ds(pl.multiple_of(i * step, step), step)
                buffer[at_rows, :] = lax.select(chosen, buffer[at_rows, :], own[at_rows, :])

            loop(parts, run)

    def group(i):
        return pl.ds(pl.multiple_of(i * 4 * xr, 4 * xr), 4 * xr)

    def forward(shared):
        for copy in shared:
            copy.wait_recv()

        def run(i):
            value = dot(routed[0, 0, group(i), :], up[pl.ds(0, wide), :])
            for ch in range(1, CHUNKS):
                value += dot(routed[0, ch, group(i), :], up[pl.ds(ch * wide, wide), :])
            sigmoid = jax.nn.sigmoid(value)
            hidden[group(i), :] = (value * sigmoid).astype(BF16)
            slope[group(i), :] = sigmoid * (1.0 + value * (1.0 - sigmoid))

        loop(2, run)

    def backward(shared):
        for copy in shared:
            copy.wait_recv()
        over_cols = ((1,), (1,))

        def run(i):
            value = dot(routed[1, 0, group(i), :], down[:, pl.ds(0, wide)], over_cols)
            for ch in range(1, CHUNKS):
                cols = pl.ds(ch * wide, wide)
                value += dot(routed[1, ch, group(i), :], down[:, cols], over_cols)
            hidden_grad[group(i), :] = (value * slope[group(i), :]).astype(BF16)

        loop(2, run)

    def parts(s, ch):
        def run(i):
            if s == 0:
                block = dot(hidden[group(i), :], down[:, pl.ds(ch * wide, wide)])
            else:
                block = dot(
                    hidden_grad[group(i), :], up[pl.ds(ch * wide, wide), :], ((1,), (1,))
                )
            part[s, ch, group(i), :] = block.astype(BF16)

        loop(2, run)
        far = part.at[s, ch, pl.ds(4 * xr, 4 * xr)]
        return start(("p", s, ch), far, core_part.at[s, ch], at(dc=1))

    def chip_sum(s, ch, copy):
        copy.wait_recv()

        def run(i):
            block = x_block_at(i)
            total = part[s, ch, block, :].astype(F32) + core_part[s, ch, block, :].astype(F32)
            part[s, ch, block, :] = total.astype(BF16)

        loop(4, run)
        return [
            start(
                ("b", s, ch, d),
                part.at[s, ch, x_block(d)],
                x_part.at[s, ch, x_block(place)],
                at(dx=NX - d),
            )
            for d, place in ((1, 1), (3, 2), (2, 0))
        ]

    def x_block_at(i):
        return pl.ds(pl.multiple_of(i * xr, xr), xr)

    def from_ring_x(s, ch, copies):
        for copy in copies:
            copy.wait_recv()
        taken = [x_part[s, ch, x_block(i), :].astype(F32) for i in range(3)]
        same_x = (part[s, ch, x_block(0), :].astype(F32) + taken[0]).astype(BF16)
        cross_x = (taken[1] + taken[2]).astype(BF16)
        block = dot(from_x[...], jnp.concatenate([same_x, cross_x], axis=0)).astype(BF16)
        got_y[s, ch] = block
        back_y[s, ch, y_block(0), :] = block[:yr]
        return [
            start(
                ("v", s, ch, d),
                got_y.at[s, ch, y_block(d)],
                back_y.at[s, ch, y_block(d)],
                at(dy=-d),
            )
            for d in range(1, ny)
        ]

    def from_ring_y(s, ch, copies):
        for copy in copies:
            copy.wait_recv()
        block = dot(from_y[...], back_y[s, ch]).astype(BF16)
        for d in range(nz):
            sent[s, ch, d] = block[d * zr : (d + 1) * zr]
        back_z[s, ch, 0] = block[:zr]
        return [
            start(("w", s, ch, d), sent.at[s, ch, d], back_z.at[s, ch, d], at(dz=-d))
            for d in range(1, nz)
        ]

    results = []

    def finish(s, ch, copies):
        for copy in copies:
            copy.wait_recv()
        block = jnp.concatenate([back_z[s, ch, d] for d in range(nz)], axis=0)
        picked = dot(unselect[...], block)
        staging, out = ((tokens, outputs), (cotangent, input_grad))[s]
        cols = pl.ds(ch * wide, wide)
        staging[:, cols] = (picked if s else weight * picked).astype(BF16)
        if ch == CHUNKS - 1:
            result = pltpu.make_async_copy(staging, out, local_sem.at[s])
            result.start()
            results.append(result)

    def up_tile(ch):
        cols = pl.ds(ch * wide, wide)
        up[cols, :] = dot(routed[0, ch], hidden_grad[...], ((0,), (0,))).astype(BF16)

    def down_tile(ch):
        cols = pl.ds(ch * wide, wide)
        down[:, cols] = dot(hidden[...], routed[1, ch], ((0,), (0,))).astype(BF16)

    def write(buffer, out, number):
        result = pltpu.make_async_copy(buffer, out, local_sem.at[number])
        result.start()
        results.append(result)

    pick(0)
    pl.semaphore_wait(barrier, len(peers))
    z_t = send_z(0)
    swaps = [
        start(("s", i), own, buffer, at(dx=1 + 2 * x_lo))
        for i, (own, buffer) in enumerate(((up_in, up), (down_in, down)))
    ]
    pick(1)
    z_g = send_z(1)
    y_t = to_ring_y(0, z_t)
    to_ring_x(0, y_t)
    x_t = send_x(0)
    y_g = to_ring_y(1, z_g)
    to_ring_x(1, y_g)
    x_g = send_x(1)
    shared_t = share(0, x_t)
    take_weights(swaps)
    settle(y_t + [x_t[1], x_t[3]])
    forward(shared_t)
    p_t = [parts(0, ch) for ch in range(CHUNKS)]
    b_t, v_t, w_t, b_g, v_g, w_g = {}, {}, {}, {}, {}, {}
    b_t[0] = chip_sum(0, 0, p_t[0])
    b_t[1] = chip_sum(0, 1, p_t[1])
    shared_g = share(1, x_g)
    settle(y_g + [x_g[1], x_g[3]])
    backward(shared_g)
    p_g = [parts(1, 0)]
    v_t[0] = from_ring_x(0, 0, b_t[0])
    b_t[2] = chip_sum(0, 2, p_t[2])
    p_g.append(parts(1, 1))
    v_t[1] = from_ring_x(0, 1, b_t[1])
    b_t[3] = chip_sum(0, 3, p_t[3])
    settle(z_t + z_g)
    w_t[0] = from_ring_y(0, 0, v_t[0])
    p_g.append(parts(1, 2))
    b_g[0] = chip_sum(1, 0, p_g[0])
    v_t[2] = from_ring_x(0, 2, b_t[2])
    w_t[1] = from_ring_y(0, 1, v_t[1])
    p_g.append(parts(1, 3))
    b_g[1] = chip_sum(1, 1, p_g[1])
    v_t[3] = from_ring_x(0, 3, b_t[3])
    w_t[2] = from_ring_y(0, 2, v_t[2])
    b_g[2] = chip_sum(1, 2, p_g[2])
    for ch in range(2):
        up_tile(ch)
    v_g[0] = from_ring_x(1, 0, b_g[0])
    w_t[3] = from_ring_y(0, 3, v_t[3])
    b_g[3] = chip_sum(1, 3, p_g[3])
    for ch in range(2, CHUNKS):
        up_tile(ch)
    write(up, up_grad, 2)
    v_g[1] = from_ring_x(1, 1, b_g[1])
    w_g[0] = from_ring_y(1, 0, v_g[0])
    finish(0, 0, w_t[0])
    for ch in range(2):
        down_tile(ch)
    v_g[2] = from_ring_x(1, 2, b_g[2])
    w_g[1] = from_ring_y(1, 1, v_g[1])
    finish(0, 1, w_t[1])
    for ch in range(2, CHUNKS):
        down_tile(ch)
    write(down, down_grad, 3)
    v_g[3] = from_ring_x(1, 3, b_g[3])
    w_g[2] = from_ring_y(1, 2, v_g[2])
    finish(0, 2, w_t[2])
    w_g[3] = from_ring_y(1, 3, v_g[3])
    finish(0, 3, w_t[3])
    for ch in range(CHUNKS):
        finish(1, ch, w_g[ch])
    settle(list(waiting.values()))
    for result in results:
        result.wait()


def shards(geo, tokens, cotangent, routes, router_probs, up_weight, down_weight, moving):
    ny, nz = geo.ny, geo.nz
    count, width = tokens.shape
    hid = up_weight.shape[2]
    rows, xr, wide = geo.rows, geo.xrows, width // CHUNKS
    vmem = pl.BlockSpec(memory_space=pltpu.VMEM)
    smem = pl.BlockSpec(memory_space=pltpu.SMEM)
    anywhere = pl.BlockSpec(memory_space=pl.ANY)
    copies = 2 * (nz - 1 + ny - 1 + 3 + 4 + CHUNKS * (1 + 3 + ny - 1 + nz - 1)) + 2
    buffer = lambda *shape: pltpu.VMEM(shape, BF16)
    outputs, input_grad, up_grad, down_grad = pl.pallas_call(
        functools.partial(kernel, geo),
        out_shape=(
            jax.ShapeDtypeStruct((count, width), BF16),
            jax.ShapeDtypeStruct((count, width), BF16),
            jax.ShapeDtypeStruct((width, hid), BF16),
            jax.ShapeDtypeStruct((hid, width), BF16),
        ),
        in_specs=[anywhere, anywhere, vmem, vmem, smem, anywhere, anywhere] + [vmem] * 4,
        out_specs=(anywhere,) * 4,
        scratch_shapes=[
            buffer(count, width),
            buffer(count, width),
            buffer(width, hid),
            buffer(hid, width),
            buffer(width, hid),
            buffer(hid, width),
            buffer(8 * xr, hid),
            buffer(8 * xr, hid),
            pltpu.VMEM((8 * xr, hid), F32),
            buffer(rows, count),
            buffer(count, rows),
            buffer(2, CHUNKS, nz, geo.zrows, wide),
            buffer(2, CHUNKS, nz, geo.zrows, wide),
            buffer(2, CHUNKS, rows, wide),
            buffer(2, CHUNKS, 8 * xr, wide),
            buffer(2, CHUNKS, 8 * xr, wide),
            buffer(2, CHUNKS, 4 * xr, wide),
            buffer(2, CHUNKS, 3 * xr, wide),
            buffer(2, CHUNKS, rows, wide),
            buffer(2, CHUNKS, nz, geo.zrows, wide),
            pltpu.SemaphoreType.DMA((copies,)),
            pltpu.SemaphoreType.DMA((copies,)),
            pltpu.SemaphoreType.DMA((4,)),
        ],
        compiler_params=pltpu.CompilerParams(
            collective_id=0, has_side_effects=True, vmem_limit_bytes=63 * 2**20
        ),
    )(
        tokens,
        cotangent,
        routes.reshape(1, count),
        router_probs.reshape(1, count),
        moving,
        up_weight[0],
        down_weight[0],
        *[jnp.asarray(m) for m in geo.matrices()],
    )
    return outputs, input_grad, up_grad[None], down_grad[None]


def solution(mesh):
    ep_count = mesh.shape["ep"]
    nz = 8 if ep_count == 64 else 2
    geo = Geometry(ep_count // 2 // nz, nz)
    in_specs = (
        P(("ep", "dp"), None),
        P(("ep", "dp"), None),
        P(("ep", "dp"), None),
        P(("ep", "dp"), None),
        P("ep", None, "dp"),
        P("ep", "dp", None),
        P(),
    )
    out_specs = (
        P(("ep", "dp"), None),
        P(("ep", "dp"), None),
        P("ep", None, "dp"),
        P("ep", "dp", None),
    )
    return jax.shard_map(
        functools.partial(shards, geo),
        mesh=mesh,
        in_specs=in_specs,
        out_specs=out_specs,
        check_vma=False,
    )
```

time: 288 us -> 239 us (0.83)
  Pallas kernels: 274 us -> 231 us
  other arithmetic: 5.75 us -> 0 us
    pallas_call x1, Pallas kernels: 274 us -> 231 us  [shards(): pl.pallas_call(functools.partial(kernel, geo), out_shape=(jax.ShapeDtypeS...]
    unnamed x11 -> x10, local copies, waits for them, and re-layouts: 8.02 us -> 6.63 us
where the time goes in v2:
time: 239 us; the launch traced here: 238 us
  Pallas kernels  231 us (97%)
  local copies, waits for them, and re-layouts  6.63 us (3%)
    pallas_call x1, Pallas kernels, shards(): pl.pallas_call(functools.partial(kernel, geo), out_shape=(jax.ShapeDtypeS...  231 us
    unnamed x10, local copies, waits for them, and re-layouts  6.63 us

profile of v2, /device:TPU:1, one launch (start us, length us, event | category | flops | bytes accessed | tf_op | source)
XLA Modules:
  0.0 238.0 jit_solution(17417156459409035877)
XLA Ops:
  0.6 230.7 %shard_map.138 = (bf16[128,3584]{1,0:T(8,128)(2,1)}, bf16[128,3584]{1,0:T(8,128)(2,1)}, bf16[3584,256]{1,0:T(8,128)(2,1)}, bf16[256,3584]{1,0:T(8,128)(2,1)}) custom-call(bf16[128,3584]{1,0:T(8,128)(2,1)} %tokens_in.1, bf16[128,3584]{1,0:T(8,128)(2,1)} %cotangent_in.1, s32[1,128]{1,0:T(1,128)} %bitcast.10, f32[1,128]{1,0:T(1,128)} %bitcast.11, s32[32]{0:T(128)} %moving.1, ...), custom_call_target="tpu_custom_call" | custom-call | tf_op jit(solution)/shard_map/pallas_call | solution.py:493
  231.3 0.0 copy-start.2
  231.4 0.0 copy-start.1
  231.4 2.3 copy.19
  233.7 0.0 copy-done.2
  233.7 0.9 copy.20
  234.6 0.0 copy-done.1
  234.6 0.0 copy-start
  234.6 1.2 copy.21
  235.8 0.9 copy-done
  236.8 1.2 copy.22
Async XLA Ops:
  231.3 2.3 copy-start.2
  231.4 3.2 %copy-start.1 = (bf16[3584,256]{1,0:T(8,128)(2,1)S(1)}, bf16[3584,256]{1,0:T(8,128)(2,1)}, u32[]{:S(2)}) copy-start(bf16[3584,256]{1,0:T(8,128)(2,1)} %get-tuple-element.10) | copy-start | bytes 5505028
  234.6 2.2 copy-start

commit v3 on v2

--- a/solution.py
+++ b/solution.py
@@ -11,7 +11,11 @@
 MESH = pl.DeviceIdType.MESH
 NX = 4
 CAP = 3
-CHUNKS = 4
+CHUNKS = 7
+LEAD = 2
+TILES = 3
+SPANS = ((0, 4), (4, 3))
+PIECES = 4
 BF16 = jnp.bfloat16
 F32 = jnp.float32
 I32 = jnp.int32
@@ -74,6 +78,8 @@
     hidden_grad,
     hidden,
     slope,
+    their_hidden,
+    their_grad,
     select,
     unselect,
     sent,
@@ -191,10 +197,9 @@
     ).astype(BF16)
     weight = as_column(probs[...])
 
-    def pick(s):
-        loads[s].wait()
-
-        def tile(ch):
+    def pick(s, first, number):
+        def tile(i):
+            ch = first + i
             cols = chunk_cols(ch)
             if s == 0:
                 given = tokens[:, cols]
@@ -205,68 +210,75 @@
                 sent[s, ch, d] = block[d * zr : (d + 1) * zr]
             got_z[s, ch, 0] = block[:zr]
 
-        loop(CHUNKS, tile)
-
-    def send_z(s):
+        loop(number, tile)
+        span = pl.ds(first, number)
         return [
-            start(("z", s, d), sent.at[s, :, d], got_z.at[s, :, d], at(dz=d)) for d in range(1, nz)
+            start(("z", s, first, d), sent.at[s, span, d], got_z.at[s, span, d], at(dz=d))
+            for d in range(1, nz)
         ]
 
-    def to_ring_y(s, copies):
+    def to_ring_y(s, first, number, copies):
         for copy in copies:
             copy.wait_recv()
 
-        def tile(ch):
+        def tile(i):
+            ch = first + i
             block = jnp.concatenate([got_z[s, ch, d] for d in range(nz)], axis=0)
             block = dot(to_y[...], block).astype(BF16)
             part[s, ch, pl.ds(0, rows), :] = block
             got_y[s, ch, y_block(0), :] = block[:yr]
 
-        loop(CHUNKS, tile)
+        loop(number, tile)
+        span = pl.ds(first, number)
         return [
             start(
-                ("y", s, d), part.at[s, :, y_block(d)], got_y.at[s, :, y_block(d)], at(dy=d)
+                ("y", s, first, d),
+                part.at[s, span, y_block(d)],
+                got_y.at[s, span, y_block(d)],
+                at(dy=d),
             )
             for d in range(1, ny)
         ]
 
-    def to_ring_x(s, copies):
+    def to_ring_x(s, first, number, copies):
         for copy in copies:
             copy.wait_recv()
 
-        def tile(ch):
+        def tile(i):
+            ch = first + i
             block = dot(to_x[...], got_y[s, ch]).astype(BF16)
             routed[s, ch, x_block(0), :] = block[:xr]
             part[s, ch, pl.ds(rows, xr), :] = block[xr:]
 
-        loop(CHUNKS, tile)
-
-    def send_x(s):
-        other = part.at[s, :, pl.ds(rows, xr)]
-        own = routed.at[s, :, x_block(0)]
+        loop(number, tile)
+        span = pl.ds(first, number)
+        other = part.at[s, span, pl.ds(rows, xr)]
+        own = routed.at[s, span, x_block(0)]
         return {
-            1: start(("x", s, 1), other, routed.at[s, :, x_block(1)], at(dx=1)),
-            3: start(("x", s, 3), other, routed.at[s, :, x_block(3)], at(dx=3)),
-            2: start(("x", s, 2), own, routed.at[s, :, x_block(2)], at(dx=2)),
-            0: start(("c", s, 0), own, routed.at[s, :, x_block(4)], at(dc=1)),
+            1: start(("x", s, first, 1), other, routed.at[s, span, x_block(1)], at(dx=1)),
+            3: start(("x", s, first, 3), other, routed.at[s, span, x_block(3)], at(dx=3)),
+            2: start(("x", s, first, 2), own, routed.at[s, span, x_block(2)], at(dx=2)),
+            0: start(("c", s, first, 0), own, routed.at[s, span, x_block(4)], at(dc=1)),
         }
 
-    def share(s, made):
+    def share(s, first, number, made):
         shared = [made[0]]
+        span = pl.ds(first, number)
         for d in (1, 3, 2):
             made[d].wait_recv()
             shared.append(
                 start(
-                    ("c", s, d),
-                    routed.at[s, :, x_block(d)],
-                    routed.at[s, :, x_block(4 + d)],
+                    ("c", s, first, d),
+                    routed.at[s, span, x_block(d)],
+                    routed.at[s, span, x_block(4 + d)],
                     at(dc=1),
                 )
             )
         return shared
 
+    chosen = moving[ep % half_count] == 1
+
     def take_weights(swaps):
-        chosen = moving[ep % half_count] == 1
         for copy, load, buffer, own, parts in zip(
             swaps, loads[2:], (up, down), (up_own, down_own), (7, 4)
         ):
@@ -310,6 +322,42 @@
             hidden_grad[group(i), :] = (value * slope[group(i), :]).astype(BF16)
 
         loop(2, run)
+
+    def traded(s):
+        mine, theirs = ((hidden, their_hidden), (hidden_grad, their_grad))[s]
+        copies = []
+        for block, other in ((0, 2), (2, 0), (4, 6), (6, 4)):
+            number = used.setdefault(("t", s, block), len(used))
+            copies.append(
+                pltpu.make_async_remote_copy(
+                    src_ref=mine.at[pl.ds(block * xr, 2 * xr)],
+                    dst_ref=theirs.at[pl.ds(other * xr, 2 * xr)],
+                    send_sem=send_sem.at[number],
+                    recv_sem=recv_sem.at[number],
+                    device_id=at(dx=2),
+                    device_id_type=MESH,
+                )
+            )
+        return copies
+
+    def trade(s):
+        @pl.when(core == 1)
+        def _():
+            for copy in traded(s):
+                copy.start()
+
+    def take_traded(s):
+        mine, theirs = ((hidden, their_hidden), (hidden_grad, their_grad))[s]
+
+        @pl.when(core == 1)
+        def _():
+            for copy in traded(s):
+                copy.wait()
+
+            def run(i):
+                mine[group(i), :] = lax.select(chosen, theirs[group(i), :], mine[group(i), :])
+
+            loop(2, run)
 
     def parts(s, ch):
         def run(i):
@@ -406,78 +454,81 @@
         result.start()
         results.append(result)
 
-    pick(0)
     pl.semaphore_wait(barrier, len(peers))
-    z_t = send_z(0)
     swaps = [
-        start(("s", i), own, buffer, at(dx=1 + 2 * x_lo))
+        start(("s", i), own, buffer, at(dx=1 + 2 * (x_lo ^ core)))
         for i, (own, buffer) in enumerate(((up_in, up), (down_in, down)))
     ]
-    pick(1)
-    z_g = send_z(1)
-    y_t = to_ring_y(0, z_t)
-    to_ring_x(0, y_t)
-    x_t = send_x(0)
-    y_g = to_ring_y(1, z_g)
-    to_ring_x(1, y_g)
-    x_g = send_x(1)
-    shared_t = share(0, x_t)
+    streams = [(s, *span) for s in range(2) for span in SPANS]
+    along_z, along_y, along_x, shared = [], [], [], ([], [])
+    for s, first, number in streams:
+        if first == 0:
+            loads[s].wait()
+        along_z.append(pick(s, first, number))
+    for stream, copies in zip(streams, along_z):
+        along_y.append(to_ring_y(*stream, copies))
+        along_x.append(to_ring_x(*stream, along_y[-1]))
+        done = len(along_x) - 3
+        if done >= 0:
+            shared[0].extend(share(*streams[done], along_x[done]))
+    from_part = [along_y[i] + [along_x[i][1], along_x[i][3]] for i in range(4)]
     take_weights(swaps)
-    settle(y_t + [x_t[1], x_t[3]])
-    forward(shared_t)
-    p_t = [parts(0, ch) for ch in range(CHUNKS)]
-    b_t, v_t, w_t, b_g, v_g, w_g = {}, {}, {}, {}, {}, {}
-    b_t[0] = chip_sum(0, 0, p_t[0])
-    b_t[1] = chip_sum(0, 1, p_t[1])
-    shared_g = share(1, x_g)
-    settle(y_g + [x_g[1], x_g[3]])
-    backward(shared_g)
-    p_g = [parts(1, 0)]
-    v_t[0] = from_ring_x(0, 0, b_t[0])
-    b_t[2] = chip_sum(0, 2, p_t[2])
-    p_g.append(parts(1, 1))
-    v_t[1] = from_ring_x(0, 1, b_t[1])
-    b_t[3] = chip_sum(0, 3, p_t[3])
-    settle(z_t + z_g)
-    w_t[0] = from_ring_y(0, 0, v_t[0])
-    p_g.append(parts(1, 2))
-    b_g[0] = chip_sum(1, 0, p_g[0])
-    v_t[2] = from_ring_x(0, 2, b_t[2])
-    w_t[1] = from_ring_y(0, 1, v_t[1])
-    p_g.append(parts(1, 3))
-    b_g[1] = chip_sum(1, 1, p_g[1])
-    v_t[3] = from_ring_x(0, 3, b_t[3])
-    w_t[2] = from_ring_y(0, 2, v_t[2])
-    b_g[2] = chip_sum(1, 2, p_g[2])
-    for ch in range(2):
-        up_tile(ch)
-    v_g[0] = from_ring_x(1, 0, b_g[0])
-    w_t[3] = from_ring_y(0, 3, v_t[3])
-    b_g[3] = chip_sum(1, 3, p_g[3])
-    for ch in range(2, CHUNKS):
-        up_tile(ch)
-    write(up, up_grad, 2)
-    v_g[1] = from_ring_x(1, 1, b_g[1])
-    w_g[0] = from_ring_y(1, 0, v_g[0])
-    finish(0, 0, w_t[0])
-    for ch in range(2):
-        down_tile(ch)
-    v_g[2] = from_ring_x(1, 2, b_g[2])
-    w_g[1] = from_ring_y(1, 1, v_g[1])
-    finish(0, 1, w_t[1])
-    for ch in range(2, CHUNKS):
-        down_tile(ch)
-    write(down, down_grad, 3)
-    v_g[3] = from_ring_x(1, 3, b_g[3])
-    w_g[2] = from_ring_y(1, 2, v_g[2])
-    finish(0, 2, w_t[2])
-    w_g[3] = from_ring_y(1, 3, v_g[3])
-    finish(0, 3, w_t[3])
-    for ch in range(CHUNKS):
-        finish(1, ch, w_g[ch])
+    settle(from_part[0] + from_part[1])
+    forward(shared[0])
+    trade(0)
+    part_sent = [parts(0, ch) for ch in range(CHUNKS)]
+    items = [(s, ch) for s in range(2) for ch in range(CHUNKS)]
+    x_given, y_given, z_given = {}, {}, {}
+    for i in range(LEAD):
+        x_given[i] = chip_sum(*items[i], part_sent[i])
+    for done in (2, 3):
+        shared[1].extend(share(*streams[done], along_x[done]))
+    settle(from_part[2] + from_part[3])
+    backward(shared[1])
+    trade(1)
+    for copies in along_z:
+        settle(copies)
+    tiles = [functools.partial(take_traded, 1)]
+    tiles += [functools.partial(up_tile, ch) for ch in range(CHUNKS)]
+    tiles += [lambda: write(up, up_grad, 2), functools.partial(take_traded, 0)]
+    tiles += [functools.partial(down_tile, ch) for ch in range(CHUNKS)]
+    tiles.append(lambda: write(down, down_grad, 3))
+    for i in range(LEAD, len(items) + LEAD + 4):
+        x_done, y_done, z_done = i - LEAD, i - LEAD - 1, i - LEAD - 4
+        if x_done in x_given:
+            y_given[x_done] = from_ring_x(*items[x_done], x_given[x_done])
+        if i < len(items):
+            x_given[i] = chip_sum(*items[i], part_sent[i])
+        if i - LEAD < CHUNKS:
+            part_sent.append(parts(1, i - LEAD))
+        if y_done in y_given:
+            z_given[y_done] = from_ring_y(*items[y_done], y_given[y_done])
+        if i - LEAD >= CHUNKS - 1:
+            for _ in range(min(TILES, len(tiles))):
+                tiles.pop(0)()
+        if z_done in z_given:
+            finish(*items[z_done], z_given[z_done])
     settle(list(waiting.values()))
     for result in results:
         result.wait()
+
+
+def place(*refs):
+    sources, targets, held, into, out_of = refs[:4], refs[4:8], refs[8:12], refs[12], refs[13]
+    loads, stores = [], []
+    for i in range(4):
+        step = sources[i].shape[0] // PIECES
+        for j in range(PIECES):
+            rows, number = pl.ds(j * step, step), PIECES * i + j
+            source, target, own = (ref[i].at[rows] for ref in (sources, targets, held))
+            loads.append(pltpu.make_async_copy(source, own, into.at[number]))
+            stores.append(pltpu.make_async_copy(own, target, out_of.at[number]))
+            loads[-1].start()
+    for load, store in zip(loads, stores):
+        load.wait()
+        store.start()
+    for store in stores:
+        store.wait()
 
 
 def shards(geo, tokens, cotangent, routes, router_probs, up_weight, down_weight, moving):
@@ -488,9 +539,10 @@
     vmem = pl.BlockSpec(memory_space=pltpu.VMEM)
     smem = pl.BlockSpec(memory_space=pltpu.SMEM)
     anywhere = pl.BlockSpec(memory_space=pl.ANY)
-    copies = 2 * (nz - 1 + ny - 1 + 3 + 4 + CHUNKS * (1 + 3 + ny - 1 + nz - 1)) + 2
+    out_copies = len(SPANS) * (nz - 1 + ny - 1 + 3 + 4)
+    copies = 2 * (out_copies + CHUNKS * (1 + 3 + ny - 1 + nz - 1) + 4) + 2
     buffer = lambda *shape: pltpu.VMEM(shape, BF16)
-    outputs, input_grad, up_grad, down_grad = pl.pallas_call(
+    results = pl.pallas_call(
         functools.partial(kernel, geo),
         out_shape=(
             jax.ShapeDtypeStruct((count, width), BF16),
@@ -510,6 +562,8 @@
             buffer(8 * xr, hid),
             buffer(8 * xr, hid),
             pltpu.VMEM((8 * xr, hid), F32),
+            buffer(8 * xr, hid),
+            buffer(8 * xr, hid),
             buffer(rows, count),
             buffer(count, rows),
             buffer(2, CHUNKS, nz, geo.zrows, wide),
@@ -538,6 +592,14 @@
         down_weight[0],
         *[jnp.asarray(m) for m in geo.matrices()],
     )
+    outputs, input_grad, up_grad, down_grad = pl.pallas_call(
+        place,
+        out_shape=[jax.ShapeDtypeStruct(r.shape, r.dtype) for r in results],
+        in_specs=[anywhere] * 4,
+        out_specs=[anywhere] * 4,
+        scratch_shapes=[pltpu.VMEM(r.shape, r.dtype) for r in results]
+        + [pltpu.SemaphoreType.DMA((4 * PIECES,))] * 2,
+    )(*results)
     return outputs, input_grad, up_grad[None], down_grad[None]
 
 

time: 239 us -> 207 us (0.87)
  Pallas kernels: 231 us -> 206 us
  local copies, waits for them, and re-layouts: 6.63 us -> 0 us
    pallas_call x1, Pallas kernels: 231 us -> 201 us  [shards(): pl.pallas_call(functools.partial(kernel, geo), out_shape=(jax.ShapeDtypeS...]
    unnamed x10 -> x0, local copies, waits for them, and re-layouts: 6.63 us -> none
    pallas_call x0 -> x1, Pallas kernels: none -> 5.05 us  [shards(): pl.pallas_call(place, out_shape=[jax.ShapeDtypeStruct(r.shape, r.dtype) f...]
where the time goes in v3:
time: 207 us
  Pallas kernels  206 us (100%)
    pallas_call x1, Pallas kernels, shards(): pl.pallas_call(functools.partial(kernel, geo), out_shape=(jax.ShapeDtypeS...  201 us
    pallas_call x1, Pallas kernels, shards(): pl.pallas_call(place, out_shape=[jax.ShapeDtypeStruct(r.shape, r.dtype) f...  5.05 us

profile of v3, /device:TPU:1, one launch (start us, length us, event | category | flops | bytes accessed | tf_op | source)
XLA Modules:
  0.0 206.9 jit_solution(1711237221993418177)
XLA Ops:
  0.6 201.1 %shard_map.138 = (bf16[128,3584]{1,0:T(8,128)(2,1)}, bf16[128,3584]{1,0:T(8,128)(2,1)}, bf16[3584,256]{1,0:T(8,128)(2,1)}, bf16[256,3584]{1,0:T(8,128)(2,1)}) custom-call(bf16[128,3584]{1,0:T(8,128)(2,1)} %tokens_in.1, bf16[128,3584]{1,0:T(8,128)(2,1)} %cotangent_in.1, s32[1,128]{1,0:T(1,128)} %bitcast.8, f32[1,128]{1,0:T(1,128)} %bitcast.9, s32[32]{0:T(128)} %moving.1, ...), custom_call_target="tpu_custom_call" | custom-call | tf_op jit(solution)/shard_map/pallas_call | solution.py:545
  201.7 5.0 %shard_map.139 = (bf16[128,3584]{1,0:T(8,128)(2,1)}, bf16[128,3584]{1,0:T(8,128)(2,1)}, bf16[3584,256]{1,0:T(8,128)(2,1)}, bf16[256,3584]{1,0:T(8,128)(2,1)}) custom-call(bf16[128,3584]{1,0:T(8,128)(2,1)} %get-tuple-element.12.refs_0_, bf16[128,3584]{1,0:T(8,128)(2,1)} %get-tuple-element.13.refs_1_, bf16[3584,256]{1,0:T(8,128)(2,1)} %get-tuple-element.14.refs_2_, ...), custom_call_target="tpu_custom_call" | custom-call | tf_op jit(solution)/shard_map/pallas_call | solution.py:595

commit v4 on v3

--- a/solution.py
+++ b/solution.py
@@ -14,8 +14,9 @@
 CHUNKS = 7
 LEAD = 2
 TILES = 3
-SPANS = ((0, 4), (4, 3))
-PIECES = 4
+SPANS = ((0, 2), (2, 5))
+PIECES = 2
+VMEM_LIMIT = 57 * 2**20
 BF16 = jnp.bfloat16
 F32 = jnp.float32
 I32 = jnp.int32
@@ -65,16 +66,12 @@
     from_y,
     to_x,
     from_x,
-    outputs,
-    input_grad,
-    up_grad,
-    down_grad,
     tokens,
     cotangent,
+    up,
+    down,
     up_own,
     down_own,
-    up,
-    down,
     hidden_grad,
     hidden,
     slope,
@@ -426,20 +423,13 @@
             for d in range(1, nz)
         ]
 
-    results = []
-
     def finish(s, ch, copies):
         for copy in copies:
             copy.wait_recv()
         block = jnp.concatenate([back_z[s, ch, d] for d in range(nz)], axis=0)
         picked = dot(unselect[...], block)
-        staging, out = ((tokens, outputs), (cotangent, input_grad))[s]
-        cols = pl.ds(ch * wide, wide)
-        staging[:, cols] = (picked if s else weight * picked).astype(BF16)
-        if ch == CHUNKS - 1:
-            result = pltpu.make_async_copy(staging, out, local_sem.at[s])
-            result.start()
-            results.append(result)
+        out = (tokens, cotangent)[s]
+        out[:, pl.ds(ch * wide, wide)] = (picked if s else weight * picked).astype(BF16)
 
     def up_tile(ch):
         cols = pl.ds(ch * wide, wide)
@@ -448,11 +438,6 @@
     def down_tile(ch):
         cols = pl.ds(ch * wide, wide)
         down[:, cols] = dot(hidden[...], routed[1, ch], ((0,), (0,))).astype(BF16)
-
-    def write(buffer, out, number):
-        result = pltpu.make_async_copy(buffer, out, local_sem.at[number])
-        result.start()
-        results.append(result)
 
     pl.semaphore_wait(barrier, len(peers))
     swaps = [
@@ -490,9 +475,8 @@
         settle(copies)
     tiles = [functools.partial(take_traded, 1)]
     tiles += [functools.partial(up_tile, ch) for ch in range(CHUNKS)]
-    tiles += [lambda: write(up, up_grad, 2), functools.partial(take_traded, 0)]
+    tiles.append(functools.partial(take_traded, 0))
     tiles += [functools.partial(down_tile, ch) for ch in range(CHUNKS)]
-    tiles.append(lambda: write(down, down_grad, 3))
     for i in range(LEAD, len(items) + LEAD + 4):
         x_done, y_done, z_done = i - LEAD, i - LEAD - 1, i - LEAD - 4
         if x_done in x_given:
@@ -509,26 +493,22 @@
         if z_done in z_given:
             finish(*items[z_done], z_given[z_done])
     settle(list(waiting.values()))
-    for result in results:
-        result.wait()
 
 
 def place(*refs):
-    sources, targets, held, into, out_of = refs[:4], refs[4:8], refs[8:12], refs[12], refs[13]
-    loads, stores = [], []
-    for i in range(4):
-        step = sources[i].shape[0] // PIECES
+    copies = []
+    for i, (source, target) in enumerate(zip(refs[:4], refs[4:8])):
+        step = source.shape[0] // PIECES
         for j in range(PIECES):
-            rows, number = pl.ds(j * step, step), PIECES * i + j
-            source, target, own = (ref[i].at[rows] for ref in (sources, targets, held))
-            loads.append(pltpu.make_async_copy(source, own, into.at[number]))
-            stores.append(pltpu.make_async_copy(own, target, out_of.at[number]))
-            loads[-1].start()
-    for load, store in zip(loads, stores):
-        load.wait()
-        store.start()
-    for store in stores:
-        store.wait()
+            rows = pl.ds(j * step, step)
+            copies.append(
+                pltpu.make_async_copy(
+                    source.at[rows], target.at[rows], refs[8].at[PIECES * i + j]
+                )
+            )
+            copies[-1].start()
+    for copy in copies:
+        copy.wait()
 
 
 def shards(geo, tokens, cotangent, routes, router_probs, up_weight, down_weight, moving):
@@ -545,18 +525,14 @@
     results = pl.pallas_call(
         functools.partial(kernel, geo),
         out_shape=(
-            jax.ShapeDtypeStruct((count, width), BF16),
-            jax.ShapeDtypeStruct((count, width), BF16),
-            jax.ShapeDtypeStruct((width, hid), BF16),
-            jax.ShapeDtypeStruct((hid, width), BF16),
-        ),
-        in_specs=[anywhere, anywhere, vmem, vmem, smem, anywhere, anywhere] + [vmem] * 4,
-        out_specs=(anywhere,) * 4,
-        scratch_shapes=[
             buffer(count, width),
             buffer(count, width),
             buffer(width, hid),
             buffer(hid, width),
+        ),
+        in_specs=[anywhere, anywhere, vmem, vmem, smem, anywhere, anywhere] + [vmem] * 4,
+        out_specs=(vmem,) * 4,
+        scratch_shapes=[
             buffer(width, hid),
             buffer(hid, width),
             buffer(8 * xr, hid),
@@ -580,7 +556,7 @@
             pltpu.SemaphoreType.DMA((4,)),
         ],
         compiler_params=pltpu.CompilerParams(
-            collective_id=0, has_side_effects=True, vmem_limit_bytes=63 * 2**20
+            collective_id=0, has_side_effects=True, vmem_limit_bytes=VMEM_LIMIT
         ),
     )(
         tokens,
@@ -597,8 +573,8 @@
         out_shape=[jax.ShapeDtypeStruct(r.shape, r.dtype) for r in results],
         in_specs=[anywhere] * 4,
         out_specs=[anywhere] * 4,
-        scratch_shapes=[pltpu.VMEM(r.shape, r.dtype) for r in results]
-        + [pltpu.SemaphoreType.DMA((4 * PIECES,))] * 2,
+        scratch_shapes=[pltpu.SemaphoreType.DMA((4 * PIECES,))],
+        compiler_params=pltpu.CompilerParams(vmem_limit_bytes=2**20),
     )(*results)
     return outputs, input_grad, up_grad[None], down_grad[None]
 

time: 207 us -> 203 us (0.981)
  Pallas kernels: 206 us -> 202 us
    pallas_call x1, Pallas kernels: 5.05 us -> 2.51 us  [shards(): pl.pallas_call(place, out_shape=[jax.ShapeDtypeStruct(r.shape, r.dtype) f...]
where the time goes in v4:
time: 203 us
  Pallas kernels  202 us (100%)
    pallas_call x1, Pallas kernels, shards(): pl.pallas_call(functools.partial(kernel, geo), out_shape=(buffer(count, w...  200 us

profile of v4, /device:TPU:1, one launch (start us, length us, event | category | flops | bytes accessed | tf_op | source)
XLA Modules:
  0.0 202.8 jit_solution(16477563620202336336)
XLA Ops:
  0.6 199.5 %shard_map.138 = (bf16[128,3584]{1,0:T(8,128)(2,1)S(1)}, bf16[128,3584]{1,0:T(8,128)(2,1)S(1)}, bf16[3584,256]{1,0:T(8,128)(2,1)S(1)}, bf16[256,3584]{1,0:T(8,128)(2,1)S(1)}) custom-call(bf16[128,3584]{1,0:T(8,128)(2,1)} %tokens_in.1, bf16[128,3584]{1,0:T(8,128)(2,1)} %cotangent_in.1, s32[1,128]{1,0:T(1,128)} %bitcast.8, f32[1,128]{1,0:T(1,128)} %bitcast.9, ...), custom_call_target="tpu_custom_call" | custom-call | tf_op jit(solution)/shard_map/pallas_call | solution.py:525
  200.2 2.5 %shard_map.139 = (bf16[128,3584]{1,0:T(8,128)(2,1)}, bf16[128,3584]{1,0:T(8,128)(2,1)}, bf16[3584,256]{1,0:T(8,128)(2,1)}, bf16[256,3584]{1,0:T(8,128)(2,1)}) custom-call(bf16[128,3584]{1,0:T(8,128)(2,1)S(1)} %get-tuple-element.12.refs_0_, bf16[128,3584]{1,0:T(8,128)(2,1)S(1)} %get-tuple-element.13.refs_1_, bf16[3584,256]{1,0:T(8,128)(2,1)S(1)} %get-tuple-element.14.refs_2_, ...), custom_call_target="tpu_custom_call" | custom-call | tf_op jit(solution)/shard_map/pallas_call | solution.py:571

commit v5 on v4

--- a/solution.py
+++ b/solution.py
@@ -432,7 +432,7 @@
         out[:, pl.ds(ch * wide, wide)] = (picked if s else weight * picked).astype(BF16)
 
     def up_tile(ch):
-        cols = pl.ds(ch * wide, wide)
+        cols = chunk_cols(ch)
         up[cols, :] = dot(routed[0, ch], hidden_grad[...], ((0,), (0,))).astype(BF16)
 
     def down_tile(ch):
@@ -470,23 +470,25 @@
         shared[1].extend(share(*streams[done], along_x[done]))
     settle(from_part[2] + from_part[3])
     backward(shared[1])
-    trade(1)
     for copies in along_z:
         settle(copies)
-    tiles = [functools.partial(take_traded, 1)]
-    tiles += [functools.partial(up_tile, ch) for ch in range(CHUNKS)]
-    tiles.append(functools.partial(take_traded, 0))
+    tiles = [functools.partial(take_traded, 0)]
     tiles += [functools.partial(down_tile, ch) for ch in range(CHUNKS)]
     for i in range(LEAD, len(items) + LEAD + 4):
         x_done, y_done, z_done = i - LEAD, i - LEAD - 1, i - LEAD - 4
         if x_done in x_given:
             y_given[x_done] = from_ring_x(*items[x_done], x_given[x_done])
+            if x_done == len(items) - 1:
+                trade(1)
         if i < len(items):
             x_given[i] = chip_sum(*items[i], part_sent[i])
         if i - LEAD < CHUNKS:
             part_sent.append(parts(1, i - LEAD))
         if y_done in y_given:
             z_given[y_done] = from_ring_y(*items[y_done], y_given[y_done])
+            if y_done == len(items) - 1:
+                take_traded(1)
+                loop(CHUNKS, up_tile)
         if i - LEAD >= CHUNKS - 1:
             for _ in range(min(TILES, len(tiles))):
                 tiles.pop(0)()

time: 203 us -> 197 us (0.970)
  Pallas kernels: 202 us -> 196 us
    pallas_call x1, Pallas kernels: 200 us -> 194 us  [shards(): pl.pallas_call(functools.partial(kernel, geo), out_shape=(buffer(count, w...]
where the time goes in v5:
time: 197 us
  Pallas kernels  196 us (99%)
    pallas_call x1, Pallas kernels, shards(): pl.pallas_call(functools.partial(kernel, geo), out_shape=(buffer(count, w...  194 us

profile of v5, /device:TPU:1, one launch (start us, length us, event | category | flops | bytes accessed | tf_op | source)
XLA Modules:
  0.0 196.8 jit_solution(4811150767918711872)
XLA Ops:
  0.6 193.7 %shard_map.138 = (bf16[128,3584]{1,0:T(8,128)(2,1)S(1)}, bf16[128,3584]{1,0:T(8,128)(2,1)S(1)}, bf16[3584,256]{1,0:T(8,128)(2,1)S(1)}, bf16[256,3584]{1,0:T(8,128)(2,1)S(1)}) custom-call(bf16[128,3584]{1,0:T(8,128)(2,1)} %tokens_in.1, bf16[128,3584]{1,0:T(8,128)(2,1)} %cotangent_in.1, s32[1,128]{1,0:T(1,128)} %bitcast.8, f32[1,128]{1,0:T(1,128)} %bitcast.9, ...), custom_call_target="tpu_custom_call" | custom-call | tf_op jit(solution)/shard_map/pallas_call | solution.py:527
  194.3 2.5 %shard_map.139 = (bf16[128,3584]{1,0:T(8,128)(2,1)}, bf16[128,3584]{1,0:T(8,128)(2,1)}, bf16[3584,256]{1,0:T(8,128)(2,1)}, bf16[256,3584]{1,0:T(8,128)(2,1)}) custom-call(bf16[128,3584]{1,0:T(8,128)(2,1)S(1)} %get-tuple-element.12.refs_0_, bf16[128,3584]{1,0:T(8,128)(2,1)S(1)} %get-tuple-element.13.refs_1_, bf16[3584,256]{1,0:T(8,128)(2,1)S(1)} %get-tuple-element.14.refs_2_, ...), custom_call_target="tpu_custom_call" | custom-call | tf_op jit(solution)/shard_map/pallas_call | solution.py:573

commit v6 on v5

--- a/solution.py
+++ b/solution.py
@@ -12,8 +12,7 @@
 NX = 4
 CAP = 3
 CHUNKS = 7
-LEAD = 2
-TILES = 3
+LEAD = 3
 SPANS = ((0, 2), (2, 5))
 PIECES = 2
 VMEM_LIMIT = 57 * 2**20
@@ -436,7 +435,7 @@
         up[cols, :] = dot(routed[0, ch], hidden_grad[...], ((0,), (0,))).astype(BF16)
 
     def down_tile(ch):
-        cols = pl.ds(ch * wide, wide)
+        cols = chunk_cols(ch)
         down[:, cols] = dot(hidden[...], routed[1, ch], ((0,), (0,))).astype(BF16)
 
     pl.semaphore_wait(barrier, len(peers))
@@ -460,7 +459,6 @@
     take_weights(swaps)
     settle(from_part[0] + from_part[1])
     forward(shared[0])
-    trade(0)
     part_sent = [parts(0, ch) for ch in range(CHUNKS)]
     items = [(s, ch) for s in range(2) for ch in range(CHUNKS)]
     x_given, y_given, z_given = {}, {}, {}
@@ -472,13 +470,12 @@
     backward(shared[1])
     for copies in along_z:
         settle(copies)
-    tiles = [functools.partial(take_traded, 0)]
-    tiles += [functools.partial(down_tile, ch) for ch in range(CHUNKS)]
     for i in range(LEAD, len(items) + LEAD + 4):
         x_done, y_done, z_done = i - LEAD, i - LEAD - 1, i - LEAD - 4
         if x_done in x_given:
             y_given[x_done] = from_ring_x(*items[x_done], x_given[x_done])
             if x_done == len(items) - 1:
+                trade(0)
                 trade(1)
         if i < len(items):
             x_given[i] = chip_sum(*items[i], part_sent[i])
@@ -487,11 +484,10 @@
         if y_done in y_given:
             z_given[y_done] = from_ring_y(*items[y_done], y_given[y_done])
             if y_done == len(items) - 1:
+                take_traded(0)
+                loop(CHUNKS, down_tile)
                 take_traded(1)
                 loop(CHUNKS, up_tile)
-        if i - LEAD >= CHUNKS - 1:
-            for _ in range(min(TILES, len(tiles))):
-                tiles.pop(0)()
         if z_done in z_given:
             finish(*items[z_done], z_given[z_done])
     settle(list(waiting.values()))

time: 197 us -> 194 us (0.985)
  Pallas kernels: 196 us -> 193 us
    pallas_call x1, Pallas kernels: 194 us -> 190 us  [shards(): pl.pallas_call(functools.partial(kernel, geo), out_shape=(buffer(count, w...]
where the time goes in v6:
time: 194 us; the launch traced here: 193 us
  Pallas kernels  193 us (99%)
    pallas_call x1, Pallas kernels, shards(): pl.pallas_call(functools.partial(kernel, geo), out_shape=(buffer(count, w...  190 us

profile of v6, /device:TPU:1, one launch (start us, length us, event | category | flops | bytes accessed | tf_op | source)
XLA Modules:
  0.0 193.3 jit_solution(4974342101054655444)
XLA Ops:
  0.6 190.2 %shard_map.138 = (bf16[128,3584]{1,0:T(8,128)(2,1)S(1)}, bf16[128,3584]{1,0:T(8,128)(2,1)S(1)}, bf16[3584,256]{1,0:T(8,128)(2,1)S(1)}, bf16[256,3584]{1,0:T(8,128)(2,1)S(1)}) custom-call(bf16[128,3584]{1,0:T(8,128)(2,1)} %tokens_in.1, bf16[128,3584]{1,0:T(8,128)(2,1)} %cotangent_in.1, s32[1,128]{1,0:T(1,128)} %bitcast.8, f32[1,128]{1,0:T(1,128)} %bitcast.9, ...), custom_call_target="tpu_custom_call" | custom-call | tf_op jit(solution)/shard_map/pallas_call | solution.py:523
  190.8 2.5 %shard_map.139 = (bf16[128,3584]{1,0:T(8,128)(2,1)}, bf16[128,3584]{1,0:T(8,128)(2,1)}, bf16[3584,256]{1,0:T(8,128)(2,1)}, bf16[256,3584]{1,0:T(8,128)(2,1)}) custom-call(bf16[128,3584]{1,0:T(8,128)(2,1)S(1)} %get-tuple-element.12.refs_0_, bf16[128,3584]{1,0:T(8,128)(2,1)S(1)} %get-tuple-element.13.refs_1_, bf16[3584,256]{1,0:T(8,128)(2,1)S(1)} %get-tuple-element.14.refs_2_, ...), custom_call_target="tpu_custom_call" | custom-call | tf_op jit(solution)/shard_map/pallas_call | solution.py:569
